TPU v7x, 512 devices: a whole 4x4x16 slice. The times are simulated.
512 devices in a mesh: gx: 16 (over x, y), gy: 8 (over z_lo), gz: 4 (over z_hi, core).
Axes of the slice: x: 4, y: 4, z: 16 (z_hi: 2, z_lo: 8; z = z_hi * 8 + z_lo), core: 2. Of those that a mesh axis runs over, the one named last changes fastest.
Arguments:
- fields: float32 [16, 192, 64, 512], P(None, 'gx', 'gy', 'gz'), may hold values from -6 to 6
- speeds: float32 [3, 16], replicated, may hold values from -1.5 to 1.5
- kinetics: float32 [16, 16], replicated, may hold values from -2 to 0.75
- block_rank: int32 [192], P('gx'), may hold values from 0 to 191, each once
- x_factor: float32 [192, 96], replicated, may hold values from -0.4375 to 0.4375
- y_factor: float32 [64, 64], P('gy'), may hold values from -0.75 to 0.75
- z_factor: float32 [512, 54], P('gz'), may hold values from -0.25 to 0.25
Outputs:
- fields_next: float32 [16, 192, 64, 512], P(None, 'gx', 'gy', 'gz')
- core: float32 [16, 96, 64, 54], P('gz', 'gx', 'gy')
Inputs may be any that keep to these rules, and one draw needn't show every extreme that they name: block_rank is a permutation of the 192 x planes.
All inputs are finite; a program needn't handle non-finite values.
Results may differ from a plain program's by a relative error of at most 0.000098.
Values sent between devices are 32-bit elements; how exact they have to be, the bound alone decides.
A program may use at most 128 MiB of HBM per device.

v0:
```python
import jax
import jax.numpy as jnp
from jax import lax
from jax.sharding import PartitionSpec as P

COEFFS = (0.8, -0.2, 4.0 / 105.0, -1.0 / 280.0)
TIME_STEP = 0.45


def with_halo(array, sides, width):
    edges = {}
    for axis, dim in sides:
        devices, length = (lax.axis_size(axis), array.shape[dim])
        up = [(i, (i + 1) % devices) for i in range(devices - 1)]
        last = lax.slice_in_dim(array, length - width, length, axis=dim)
        initial = lax.slice_in_dim(array, 0, width, axis=dim)
        edges[dim] = (
            lax.ppermute(last, axis, up),
            lax.ppermute(initial, axis, [(b, a) for a, b in up]),
        )
    done = []
    for _, dim in sides:
        low, high = edges[dim]
        around = [(width, width) if d in done else (0, 0) for d in range(array.ndim)]
        array = jnp.concatenate([jnp.pad(low, around), array, jnp.pad(high, around)], axis=dim)
        done.append(dim)
    return array


def cut_along(array, dim, devices):
    before, after = (array.shape[:dim], array.shape[dim + 1 :])
    return jnp.moveaxis(array.reshape(*before, devices, -1, *after), dim, 0)


def sent_and_summed(array, axis, dim):
    pieces = cut_along(array, dim, lax.axis_size(axis))
    arrived = lax.all_to_all(pieces, axis, split_axis=0, concat_axis=0, tiled=True)
    return arrived.sum(axis=0)


def tendency(padded, speeds, kinetics):
    extent = [padded.shape[1] - 8, padded.shape[2] - 8, padded.shape[3] - 8]

    def window(direction, offset):
        starts = [4, 4, 4]
        starts[direction] = starts[direction] + offset
        return padded[
            :,
            starts[0] : starts[0] + extent[0],
            starts[1] : starts[1] + extent[1],
            starts[2] : starts[2] + extent[2],
        ]

    center = window(0, 0)
    result = jnp.einsum("vw,wxyz->vxyz", kinetics, center, precision=lax.Precision.HIGHEST)
    for direction in range(3):
        gradient = COEFFS[0] * (window(direction, 1) - window(direction, -1))
        for offset in range(2, 5):
            gradient = gradient + COEFFS[offset - 1] * (
                window(direction, offset) - window(direction, -offset)
            )
        result = result - speeds[direction][:, None, None, None] * gradient
    return result


def shallow_rim(values):
    return with_halo(values, (("gx", 1), ("gy", 2), ("gz", 3)), 4)


def local(fields, speeds, kinetics, block_rank, x_factor, y_factor, z_factor):
    section = fields + TIME_STEP * tendency(shallow_rim(fields), speeds, kinetics)
    fields_next = 0.5 * (
        fields + section + TIME_STEP * tendency(shallow_rim(section), speeds, kinetics)
    )
    hp = lax.Precision.HIGHEST
    plane_ids = jnp.arange(x_factor.shape[0], dtype=jnp.int32)
    selector = (block_rank[:, None] == plane_ids[None, :]).astype(jnp.float32)
    x_rows = jnp.dot(selector, x_factor, precision=hp, preferred_element_type=jnp.float32)
    partial_z = jnp.einsum("vxyz,zc->vxyc", fields_next, z_factor, precision=hp)
    summed_z = sent_and_summed(partial_z, "gz", 0)
    partial_x = jnp.einsum("vxyc,xa->vayc", summed_z, x_rows, precision=hp)
    summed_x = sent_and_summed(partial_x, "gx", 1)
    partial_y = jnp.einsum("vayc,yb->vabc", summed_x, y_factor, precision=hp)
    core = sent_and_summed(partial_y, "gy", 2)
    return (fields_next, core)


def solution(mesh):
    placed = (P(None, "gx", "gy", "gz"), P(), P(), P("gx"), P(), P("gy", None), P("gz", None))
    return jax.shard_map(
        local,
        mesh=mesh,
        in_specs=placed,
        out_specs=(P(None, "gx", "gy", "gz"), P("gz", "gx", "gy", None)),
        check_vma=False,
    )
```

profile of v0, /device:TPU:6, one launch (start us, length us, event | category | flops | bytes accessed | tf_op | source)
XLA Modules:
  0.0 212.2 jit_solution(7975771367153829059)
XLA Ops:
  0.7 1.1 fusion.91
  1.8 0.9 copy.78
  2.7 3.5 %collective-permute-start.1 = (f32[16,4,8,128]{3,0,2,1:T(8,128)}, f32[16,4,8,128]{3,0,2,1:T(8,128)}, u32[]{:S(2)}, u32[]{:S(2)}) collective-permute-start(f32[16,4,8,128]{3,0,2,1:T(8,128)} %copy.78), channel_id=1, source_target_pairs={{0,32},{32,64},{64,96},{96,128},{128,160},{160,192},{192,224},{224... | collective-permute-start | bytes 786440 | tf_op jit(solution)/shard_map/ppermute | solution.py:18
  6.2 0.9 copy.79
  7.0 4.5 %collective-permute-start = (f32[16,4,8,128]{3,0,2,1:T(8,128)}, f32[16,4,8,128]{3,0,2,1:T(8,128)S(1)}, u32[]{:S(2)}, u32[]{:S(2)}) collective-permute-start(f32[16,4,8,128]{3,0,2,1:T(8,128)} %copy.79), channel_id=1, source_target_pairs={{32,0},{64,32},{96,64},{128,96},{160,128},{192,160},{224,192},{256... | collective-permute-start | bytes 786440 | tf_op jit(solution)/shard_map/ppermute | solution.py:19
  11.5 1.6 fusion.90
  13.2 4.6 %collective-permute-start.3 = (f32[16,12,4,128]{3,0,2,1:T(8,128)S(1)}, f32[16,12,4,128]{3,0,2,1:T(8,128)}, u32[]{:S(2)}, u32[]{:S(2)}) collective-permute-start(f32[16,12,4,128]{3,0,2,1:T(8,128)S(1)} %copy.80), channel_id=1, source_target_pairs={{0,4},{4,8},{8,12},{12,16},{16,20},{20,24},{24,28},{1,5},{5,9},{9,... | collective-permute-start | bytes 1179656 | tf_op jit(solution)/shard_map/ppermute | solution.py:18
  17.8 0.3 fusion.89
  18.1 1.3 copy.68
  19.4 1.3 collective-permute-start.4
  20.7 0.7 copy.69
  21.4 3.7 %collective-permute-start.5 = (f32[16,12,8,4]{0,2,3,1:T(8,128)S(1)}, f32[16,12,8,4]{0,2,3,1:T(8,128)}, u32[]{:S(2)}, u32[]{:S(2)}) collective-permute-start(f32[16,12,8,4]{0,2,3,1:T(8,128)S(1)} %copy.69), channel_id=1, source_target_pairs={{0,1},{1,2},{2,3},{4,5},{5,6},{6,7},{8,9},{9,10},{10,11},{12,13},{... | collective-permute-start | bytes 73736 | tf_op jit(solution)/shard_map/ppermute | solution.py:18
  25.1 0.9 copy.81
  26.0 1.3 collective-permute-start.2
  27.2 0.6 copy.48
  27.9 1.6 copy.50
  29.4 1.0 constant_dynamic-update-slice_fusion.3
  30.4 0.5 constant_dynamic-update-slice_fusion.1
  31.0 1.1 pad.27
  32.1 3.7 %collective-permute-done.2 = f32[16,12,4,128]{3,0,2,1:T(8,128)S(1)} collective-permute-done((f32[16,12,4,128]{3,0,2,1:T(8,128)}, f32[16,12,4,128]{3,0,2,1:T(8,128)S(1)}, u32[]{:S(2)}, u32[]{:S(2)}) %collective-permute-start.2) | collective-permute-done | bytes 393248 | tf_op jit(solution)/shard_map/ppermute | solution.py:19
  35.9 2.7 %select_maximum_fusion.3 = (f32[16,20,16,132]{3,0,2,1:T(8,128)S(1)}, f32[16,20,16,132]{3,0,2,1:T(8,128)S(1)}) fusion(f32[16,12,8,4]{3,0,2,1:T(8,128)S(1)} %copy.48, f32[16,20,4,128]{3,0,2,1:T(8,128)S(1)} %pad.26, f32[16,20,8,128]{3,0,2,1:T(8,128)S(1)} %get-tuple-element.30, f32[16,20,4,128]{3,0,2,1:T(8,128)S(1)} %pad.27, f32[16,12,8,4]{3,0,2,1:T(8,128)S(1)} %copy.50), kind=kLoop, calls=%fused_computation.4 | loop fusion | flops 6758400 | bytes 8077312 | tf_op jit(solution)/shard_map/concatenate | solution.py:25
  38.6 2.6 %fusion.9 = f32[16,12,8,128]{3,0,2,1:T(8,128)S(1)} fusion(f32[16,20,8,128]{3,0,2,1:T(8,128)S(1)} %get-tuple-element.30, f32[16,20,4,128]{3,0,2,1:T(8,128)S(1)} %pad.27, f32[16,20,4,128]{3,0,2,1:T(8,128)S(1)} %pad.26, f32[16,20,16,132]{3,0,2,1:T(8,128)S(1)} %get-tuple-element.11, f32[16,20,16,132]{3,0,2,1:T(8,128)S(1)} %get-tuple-element.10, ...), kind=kOutput, calls=%fused_computation.38 | convolution fusion | flops 47382528 | bytes 17573376 | tf_op jit(solution)/shard_map/vw,wxyz->vxyz/dot_general | solution.py:55
  41.2 0.9 fusion.87
  42.2 1.3 collective-permute-start.8
  43.4 5.8 %collective-permute-start.9 = (f32[16,12,4,128]{3,0,2,1:T(8,128)}, f32[16,12,4,128]{3,0,2,1:T(8,128)}, u32[]{:S(2)}, u32[]{:S(2)}) collective-permute-start(f32[16,12,4,128]{3,0,2,1:T(8,128)} %get-tuple-element.16), channel_id=1, source_target_pairs={{0,4},{4,8},{8,12},{12,16},{16,20},{20,24},{24,28},{1,5},{5,9},{9,... | collective-permute-start | bytes 1179656 | tf_op jit(solution)/shard_map/ppermute | solution.py:18
  49.2 0.9 fusion.88
  50.1 1.9 collective-permute-start.7
  52.0 6.0 %collective-permute-start.6 = (f32[16,4,8,128]{3,0,2,1:T(8,128)}, f32[16,4,8,128]{3,0,2,1:T(8,128)}, u32[]{:S(2)}, u32[]{:S(2)}) collective-permute-start(f32[16,4,8,128]{3,0,2,1:T(8,128)} %get-tuple-element.18), channel_id=1, source_target_pairs={{32,0},{64,32},{96,64},{128,96},{160,128},{192,160},{224,192},{256... | collective-permute-start | bytes 786440 | tf_op jit(solution)/shard_map/ppermute | solution.py:19
  58.1 0.3 fusion.86
  58.3 1.3 copy.53
  59.7 1.3 collective-permute-start.10
  61.0 0.6 copy.55
  61.6 20.2 %collective-permute-done.10 = f32[16,12,8,4]{0,2,3,1:T(8,128)S(1)} collective-permute-done((f32[16,12,8,4]{0,2,3,1:T(8,128)}, f32[16,12,8,4]{0,2,3,1:T(8,128)S(1)}, u32[]{:S(2)}, u32[]{:S(2)}) %collective-permute-start.10) | collective-permute-done | bytes 24608 | tf_op jit(solution)/shard_map/ppermute | solution.py:19
  81.8 15.4 %collective-permute-start.11 = (f32[16,12,8,4]{0,2,3,1:T(8,128)S(1)}, f32[16,12,8,4]{0,2,3,1:T(8,128)}, u32[]{:S(2)}, u32[]{:S(2)}) collective-permute-start(f32[16,12,8,4]{0,2,3,1:T(8,128)S(1)} %copy.55), channel_id=1, source_target_pairs={{0,1},{1,2},{2,3},{4,5},{5,6},{6,7},{8,9},{9,10},{10,11},{12,13},{... | collective-permute-start | bytes 73736 | tf_op jit(solution)/shard_map/ppermute | solution.py:18
  97.2 0.6 copy.54
  97.9 1.6 copy.56
  99.4 1.1 pad.30
  100.5 1.1 pad.31
  101.6 1.5 pad_maximum_fusion
  103.1 4.3 %select_maximum_fusion.1 = (f32[16,20,16,132]{3,0,2,1:T(8,128)S(1)}, f32[16,20,16,132]{3,0,2,1:T(8,128)S(1)}) fusion(f32[16,12,8,4]{3,0,2,1:T(8,128)S(1)} %copy.54, f32[16,20,4,128]{3,0,2,1:T(8,128)S(1)} %pad.30, f32[16,4,8,128]{3,0,2,1:T(8,128)} %collective-permute-done.6, f32[16,12,8,128]{3,0,2,1:T(8,128)S(1)} %fusion.9, ...), kind=kLoop, calls=%fused_computation.1 | loop fusion | flops 9461760 | bytes 8077312 | tf_op jit(solution)/shard_map/concatenate | solution.py:25
  107.5 3.5 %fusion.5 = f32[16,12,8,128]{3,0,2,1:T(8,128)S(1)} fusion(f32[16,12,8,128]{3,0,2,1:T(8,128)S(1)} %fusion.9, f32[16,4,8,128]{3,0,2,1:T(8,128)S(1)} %collective-permute-done.7, f32[16,4,8,128]{3,0,2,1:T(8,128)} %collective-permute-done.6, f32[16,20,16,132]{3,0,2,1:T(8,128)S(1)} %get-tuple-element.9, f32[16,20,16,132]{3,0,2,1:T(8,128)S(1)} %get-tuple-element.8, ...), kind=kOutput, calls=%fused_computation.34 | convolution fusion | flops 47775744 | bytes 16262656 | tf_op jit(solution)/shard_map/vw,wxyz->vxyz/dot_general | solution.py:55
  111.0 0.3 copy.63
  111.3 0.9 copy-done.2
  112.1 0.8 fusion.79
  112.9 1.7 reshape.24
  114.6 13.9 %all-to-all-start = ((f32[4,1,20736]{2,1,0:T(1,128)}), f32[4,1,20736]{2,1,0:T(1,128)S(1)}, u32[]{:S(2)}, u32[]{:S(2)}) async-start(f32[4,1,20736]{2,1,0:T(1,128)} %reshape.24), calls=%async_computation | async-start | bytes 663552 | tf_op jit(solution)/shard_map/all_to_all | solution.py:37
  128.5 0.2 convolution_bitcast_fusion.3
  128.7 22.2 %all-to-all-done = f32[4,1,20736]{2,1,0:T(1,128)S(1)} async-done(((f32[4,1,20736]{2,1,0:T(1,128)}), f32[4,1,20736]{2,1,0:T(1,128)S(1)}, u32[]{:S(2)}, u32[]{:S(2)}) %all-to-all-start) | async-done | bytes 331808 | tf_op jit(solution)/shard_map/all_to_all | solution.py:37
  150.9 0.5 broadcast.63
  151.4 1.6 reduce
  153.0 1.1 reshape.25
  154.2 1.6 convolution_bitcast_fusion
  155.8 0.6 copy.59
  156.6 2.2 %reshape.26 = f32[16,1,10368]{2,1,0:T(1,128)S(1)} reshape(f32[16,4,6,8,54]{4,3,2,1,0:T(8,128)S(1)} %copy.60) | data formatting | bytes 1327104
  158.8 13.3 %all_to_all.15 = f32[16,1,10368]{2,1,0:T(1,128)S(1)} all-to-all(f32[16,1,10368]{2,1,0:T(1,128)S(1)} %reshape.26), channel_id=1, replica_groups=mesh['gx'=16,'gy'=8,'gz'=4] {'gx'}, dimensions={0} | all-to-all | bytes 1327104 | tf_op jit(solution)/shard_map/all_to_all | solution.py:37
  172.1 2.2 %reduce.1 = f32[16,10368]{1,0:T(8,128)S(1)} reduce(f32[16,1,10368]{2,1,0:T(1,128)S(1)} %all_to_all.15, f32[]{:T(128)} %broadcast.63), dimensions={1}, to_apply=%all_to_all.10.reduce_sub_computation | reduce | bytes 1327108 | tf_op jit(solution)/shard_map/all_to_all | solution.py:37
  174.3 2.2 %reshape.27 = f32[16,4,6,8,54]{4,3,2,1,0:T(8,128)S(1)} reshape(f32[16,10368]{1,0:T(8,128)S(1)} %reduce.1) | data formatting | bytes 1327104
  176.6 1.3 convolution_bitcast_fusion.2
  177.9 0.3 copy.61
  178.3 1.0 reshape.28
  179.3 29.7 %all_to_all.16 = f32[8,1,10368]{2,1,0:T(1,128)S(1)} all-to-all(f32[8,1,10368]{2,1,0:T(1,128)S(1)} %reshape.28), channel_id=1, replica_groups=mesh['gx'=16,'gy'=8,'gz'=4] {'gy'}, dimensions={0} | all-to-all | bytes 663552 | tf_op jit(solution)/shard_map/all_to_all | solution.py:37
  209.0 1.4 reduce.2
  210.4 1.0 reshape.29
  211.5 0.7 reduce_sum.29
  (33 shorter events, 0.7 us)
Async XLA Ops:
  0.6 127.9 %copy-start = (f32[192,96]{1,0:T(8,128)S(1)}, f32[192,96]{1,0:T(8,128)}, u32[]{:S(2)}) copy-start(f32[192,96]{1,0:T(8,128)} %param.11) | copy-start | bytes 221188
  0.6 17.1 %copy-start.1 = (f32[16,12,8,128]{3,2,1,0:T(8,128)S(1)}, f32[16,12,8,128]{3,2,1,0:T(8,128)}, u32[]{:S(2)}) copy-start(f32[16,12,8,128]{3,2,1,0:T(8,128)} %param.7) | copy-start | bytes 2359300
  0.7 24.4 %copy-start.5 = (f32[3,16]{1,0:T(4,128)S(1)}, f32[3,16]{1,0:T(4,128)}, u32[]{:S(2)}) copy-start(f32[3,16]{1,0:T(4,128)} %param.8) | copy-start | bytes 580
  2.7 26.8 %collective-permute-start.1 = (f32[16,4,8,128]{3,0,2,1:T(8,128)}, f32[16,4,8,128]{3,0,2,1:T(8,128)}, u32[]{:S(2)}, u32[]{:S(2)}) collective-permute-start(f32[16,4,8,128]{3,0,2,1:T(8,128)} %copy.78), channel_id=1, source_target_pairs={{0,32},{32,64},{64,96},{96,128},{128,160},{160,192},{192,224},{224... | collective-permute-start | bytes 786440 | tf_op jit(solution)/shard_map/ppermute | solution.py:18
  7.0 23.9 %collective-permute-start = (f32[16,4,8,128]{3,0,2,1:T(8,128)}, f32[16,4,8,128]{3,0,2,1:T(8,128)S(1)}, u32[]{:S(2)}, u32[]{:S(2)}) collective-permute-start(f32[16,4,8,128]{3,0,2,1:T(8,128)} %copy.79), channel_id=1, source_target_pairs={{32,0},{64,32},{96,64},{128,96},{160,128},{192,160},{224,192},{256... | collective-permute-start | bytes 786440 | tf_op jit(solution)/shard_map/ppermute | solution.py:19
  13.2 17.8 %collective-permute-start.3 = (f32[16,12,4,128]{3,0,2,1:T(8,128)S(1)}, f32[16,12,4,128]{3,0,2,1:T(8,128)}, u32[]{:S(2)}, u32[]{:S(2)}) collective-permute-start(f32[16,12,4,128]{3,0,2,1:T(8,128)S(1)} %copy.80), channel_id=1, source_target_pairs={{0,4},{4,8},{8,12},{12,16},{16,20},{20,24},{24,28},{1,5},{5,9},{9,... | collective-permute-start | bytes 1179656 | tf_op jit(solution)/shard_map/ppermute | solution.py:18
  19.4 6.6 %collective-permute-start.4 = (f32[16,12,8,4]{0,2,3,1:T(8,128)}, f32[16,12,8,4]{0,2,3,1:T(8,128)S(1)}, u32[]{:S(2)}, u32[]{:S(2)}) collective-permute-start(f32[16,12,8,4]{0,2,3,1:T(8,128)} %copy.68), channel_id=1, source_target_pairs={{1,0},{2,1},{3,2},{5,4},{6,5},{7,6},{9,8},{10,9},{11,10},{13,12},{... | collective-permute-start | bytes 73736 | tf_op jit(solution)/shard_map/ppermute | solution.py:19
  21.4 6.5 %collective-permute-start.5 = (f32[16,12,8,4]{0,2,3,1:T(8,128)S(1)}, f32[16,12,8,4]{0,2,3,1:T(8,128)}, u32[]{:S(2)}, u32[]{:S(2)}) collective-permute-start(f32[16,12,8,4]{0,2,3,1:T(8,128)S(1)} %copy.69), channel_id=1, source_target_pairs={{0,1},{1,2},{2,3},{4,5},{5,6},{6,7},{8,9},{9,10},{10,11},{12,13},{... | collective-permute-start | bytes 73736 | tf_op jit(solution)/shard_map/ppermute | solution.py:18
  26.0 9.9 %collective-permute-start.2 = (f32[16,12,4,128]{3,0,2,1:T(8,128)}, f32[16,12,4,128]{3,0,2,1:T(8,128)S(1)}, u32[]{:S(2)}, u32[]{:S(2)}) collective-permute-start(f32[16,12,4,128]{3,0,2,1:T(8,128)} %copy.81), channel_id=1, source_target_pairs={{4,0},{8,4},{12,8},{16,12},{20,16},{24,20},{28,24},{5,1},{9,5},{13... | collective-permute-start | bytes 1179656 | tf_op jit(solution)/shard_map/ppermute | solution.py:19
  35.9 2.7 %copy-start.7 = (f32[16,16]{1,0:T(8,128)S(1)}, f32[16,16]{1,0:T(8,128)}, u32[]{:S(2)}) copy-start(f32[16,16]{1,0:T(8,128)} %param.9) | copy-start | bytes 3076
  42.2 57.3 %collective-permute-start.8 = (f32[16,12,4,128]{3,0,2,1:T(8,128)}, f32[16,12,4,128]{3,0,2,1:T(8,128)}, u32[]{:S(2)}, u32[]{:S(2)}) collective-permute-start(f32[16,12,4,128]{3,0,2,1:T(8,128)} %get-tuple-element.17), channel_id=1, source_target_pairs={{4,0},{8,4},{12,8},{16,12},{20,16},{24,20},{28,24},{5,1},{9,5},{13... | collective-permute-start | bytes 1179656 | tf_op jit(solution)/shard_map/ppermute | solution.py:19
  43.4 57.0 %collective-permute-start.9 = (f32[16,12,4,128]{3,0,2,1:T(8,128)}, f32[16,12,4,128]{3,0,2,1:T(8,128)}, u32[]{:S(2)}, u32[]{:S(2)}) collective-permute-start(f32[16,12,4,128]{3,0,2,1:T(8,128)} %get-tuple-element.16), channel_id=1, source_target_pairs={{0,4},{4,8},{8,12},{12,16},{16,20},{20,24},{24,28},{1,5},{5,9},{9,... | collective-permute-start | bytes 1179656 | tf_op jit(solution)/shard_map/ppermute | solution.py:18
  50.1 51.4 %collective-permute-start.7 = (f32[16,4,8,128]{3,0,2,1:T(8,128)}, f32[16,4,8,128]{3,0,2,1:T(8,128)S(1)}, u32[]{:S(2)}, u32[]{:S(2)}) collective-permute-start(f32[16,4,8,128]{3,0,2,1:T(8,128)} %get-tuple-element.19), channel_id=1, source_target_pairs={{0,32},{32,64},{64,96},{96,128},{128,160},{160,192},{192,224},{224... | collective-permute-start | bytes 786440 | tf_op jit(solution)/shard_map/ppermute | solution.py:18
  52.0 49.5 %collective-permute-start.6 = (f32[16,4,8,128]{3,0,2,1:T(8,128)}, f32[16,4,8,128]{3,0,2,1:T(8,128)}, u32[]{:S(2)}, u32[]{:S(2)}) collective-permute-start(f32[16,4,8,128]{3,0,2,1:T(8,128)} %get-tuple-element.18), channel_id=1, source_target_pairs={{32,0},{64,32},{96,64},{128,96},{160,128},{192,160},{224,192},{256... | collective-permute-start | bytes 786440 | tf_op jit(solution)/shard_map/ppermute | solution.py:19
  59.7 22.1 %collective-permute-start.10 = (f32[16,12,8,4]{0,2,3,1:T(8,128)}, f32[16,12,8,4]{0,2,3,1:T(8,128)S(1)}, u32[]{:S(2)}, u32[]{:S(2)}) collective-permute-start(f32[16,12,8,4]{0,2,3,1:T(8,128)} %copy.53), channel_id=1, source_target_pairs={{1,0},{2,1},{3,2},{5,4},{6,5},{7,6},{9,8},{10,9},{11,10},{13,12},{... | collective-permute-start | bytes 73736 | tf_op jit(solution)/shard_map/ppermute | solution.py:19
  81.8 16.1 %collective-permute-start.11 = (f32[16,12,8,4]{0,2,3,1:T(8,128)S(1)}, f32[16,12,8,4]{0,2,3,1:T(8,128)}, u32[]{:S(2)}, u32[]{:S(2)}) collective-permute-start(f32[16,12,8,4]{0,2,3,1:T(8,128)S(1)} %copy.55), channel_id=1, source_target_pairs={{0,1},{1,2},{2,3},{4,5},{5,6},{6,7},{8,9},{9,10},{10,11},{12,13},{... | collective-permute-start | bytes 73736 | tf_op jit(solution)/shard_map/ppermute | solution.py:18
  107.4 4.7 %copy-start.3 = (f32[128,54]{0,1:T(8,128)S(1)}, f32[128,54]{0,1:T(8,128)}, u32[]{:S(2)}) copy-start(f32[128,54]{0,1:T(8,128)} %param.13) | copy-start | bytes 82948
  107.5 21.0 %copy-start.6 = (s32[12]{0:T(128)S(1)}, s32[12]{0:T(128)}, u32[]{:S(2)}) copy-start(s32[12]{0:T(128)} %param.10) | copy-start | bytes 148
  111.3 0.9 copy-start.2
  114.6 36.3 %all-to-all-start = ((f32[4,1,20736]{2,1,0:T(1,128)}), f32[4,1,20736]{2,1,0:T(1,128)S(1)}, u32[]{:S(2)}, u32[]{:S(2)}) async-start(f32[4,1,20736]{2,1,0:T(1,128)} %reshape.24), calls=%async_computation | async-start | bytes 663552 | tf_op jit(solution)/shard_map/all_to_all | solution.py:37
  156.4 20.2 %copy-start.4 = (f32[8,64]{1,0:T(8,128)S(1)}, f32[8,64]{1,0:T(8,128)}, u32[]{:S(2)}) copy-start(f32[8,64]{1,0:T(8,128)} %param.12) | copy-start | bytes 6148
where the time goes:
time: 214 us; the launch traced here: 212 us
  starting transfers between devices  64.4 us (30%)
  waiting for transfers between devices  46.2 us (22%)
  blocking collectives  43 us (20%)
  local copies, waits for them, and re-layouts  33 us (15%)
  other arithmetic  14.6 us (7%)
  matrix products  9.96 us (5%)
    all_to_all x2, blocking collectives, sent_and_summed(): lax.all_to_all(pieces, axis, split_axis=0, concat_axis=0, tiled=True)  43 us
    ppermute x6, starting transfers between devices, with_halo(): lax.ppermute(last, axis, up)  34.9 us
    ppermute x6, waiting for transfers between devices, with_halo(): lax.ppermute(initial, axis, [(b, a) for a, b in up])  23.9 us
    all_to_all x1, waiting for transfers between devices, sent_and_summed(): lax.all_to_all(pieces, axis, split_axis=0, concat_axis=0, tiled=True)  22.2 us
    unnamed x31, local copies, waits for them, and re-layouts  16.7 us
    ppermute x6, starting transfers between devices, with_halo(): lax.ppermute(initial, axis, [(b, a) for a, b in up])  15.6 us
    all_to_all x1, starting transfers between devices, sent_and_summed(): lax.all_to_all(pieces, axis, split_axis=0, concat_axis=0, tiled=True)  13.9 us
    concatenate x3, other arithmetic, with_halo(): jnp.concatenate([jnp.pad(low, around), array, jnp.pad(high, around)], axi...  8.54 us
  transfers between devices with their start and end apart: 13, of which 3 were waited for; matrix products, arithmetic and copies ran while one was open for 9% of the time, Pallas kernels for 0%

commit v1 on v0

v1 whole, which is shorter than its diff:
```python
import jax
import jax.numpy as jnp
from jax import lax
from jax.experimental import pallas as pl
from jax.experimental.pallas import tpu as pltpu
from jax.sharding import PartitionSpec as P

COEFFS = (0.8, -0.2, 4.0 / 105.0, -1.0 / 280.0)
TIME_STEP = 0.45
MESH = pl.DeviceIdType.MESH
f32, bf16 = jnp.float32, jnp.bfloat16
NN = (((1,), (0,)), ((), ()))
NT = (((1,), (1,)), ((), ()))
TN = (((0,), (0,)), ((), ()))


def dot(a, b, dims=NN):
    return lax.dot_general(a, b, dims, preferred_element_type=f32)


def split(a):
    high = a.astype(bf16)
    return high, (a - high.astype(f32)).astype(bf16)


def iota(shape, dim):
    return lax.broadcasted_iota(jnp.int32, shape, dim)


def onehot(mask):
    return jnp.where(mask, 1.0, 0.0).astype(bf16)


def stencil(offset):
    value = jnp.zeros(offset.shape, f32)
    for k, c in enumerate(COEFFS):
        value = jnp.where(offset == k + 1, c, value)
        value = jnp.where(offset == -k - 1, -c, value)
    return value


def quadrants(t):
    m, n = t.shape[0] // 2, t.shape[1] // 2
    return t[:m, :n] + (t[m:, :n] + t[:m, n:])


def halves(t):
    n = t.shape[1] // 2
    return t[:, :n] + t[:, n:]


def both(a):
    return jnp.concatenate(split(a), axis=1)


def kernel(
    f_ref, speeds_ref, kin_ref, rank_ref, xf_ref, yf_ref, zf_ref,
    next_ref, core_ref,
    FX, SX, YB, ZS, ZB, FN, PB, BR, QB, CT, RB, EU, FU, SB, GB, XR, XG, YT, YG, ZP,
    A2, D2, E2, SEL, Z2, X2, W2, SXR, SZR,
    load_sem, out_sem, own_sem, ysend, yrecv, zsend, zrecv, z0send, z0recv, xsend, xrecv,
    bsend, brecv, csend, crecv, esend, erecv, fsend, frecv, gsend, grecv,
    xrs, xrr, yrs, yrr,
):
    g, l, q = lax.axis_index("gx"), lax.axis_index("gy"), lax.axis_index("gz")
    h, k = q // 2, lax.rem(q, 2)
    ring = h * 8 + l
    partner = q + 1 - 2 * k

    def ring_device(r):
        return (g, lax.rem(r, 8), 2 * (r // 8) + k)

    def remote(src, dst, send, recv, device):
        return pltpu.make_async_remote_copy(
            src_ref=src, dst_ref=dst, send_sem=send, recv_sem=recv,
            device_id=device, device_id_type=MESH)

    def load(x):
        return pltpu.make_async_copy(f_ref.at[:, x], FX.at[4 + x], load_sem.at[x])

    def ycopy(s, d, p):
        X = (FX, SX)[s]
        rows = pl.ds(4 * d, 4)
        return remote(X.at[4 + p, :, rows], YB.at[s, p, :, rows], ysend.at[s, d, p],
                      yrecv.at[s, d, p], (g, l + 2 * d - 1, q))

    def z0copy(d):
        rows = pl.ds(4 * d, 4)
        return remote(ZS.at[0, :, rows], ZB.at[0, :, rows], z0send.at[d], z0recv.at[d],
                      (g, l, q + 2 * d - 1))

    def zcopy(d, p):
        rows = pl.ds(4 * d, 4)
        return remote(ZS.at[1, p, rows], ZB.at[1, p, rows], zsend.at[d, p], zrecv.at[d, p],
                      (g, l, q + 2 * d - 1))

    def xcopy(s, d, i):
        X = (FX, SX)[s]
        src, dst = (12 + i, i) if d else (4 + i, 16 + i)
        return remote(X.at[src], X.at[dst], xsend.at[s, d, i], xrecv.at[s, d, i],
                      (g + 2 * d - 1, l, q))

    def bcopy(x):
        return remote(PB.at[1 - k, x], BR.at[x], bsend.at[x], brecv.at[x], (g, l, partner))

    def can_send(index, last, d):
        return index < last if d else index > 0

    def can_recv(index, last, d):
        return index > 0 if d else index < last

    for x in range(12):
        load(x).start()

    barrier = pltpu.get_barrier_semaphore()

    def greet(device):
        pl.semaphore_signal(barrier, inc=1, device_id=device, device_id_type=MESH)

    far = jnp.logical_or(q == 1, q == 2)

    def greet_others(i, c):
        greet((lax.rem(g + i, 16), l, q))
        greet(ring_device(lax.rem(ring + i, 16)))
        return c

    greet((g, l, partner))
    lax.fori_loop(1, 16, greet_others, 0)

    @pl.when(far)
    def _():
        greet((g, l, 3 - q))

    for d in range(2):
        rows = pl.ds(4 * d, 4)

        @pl.when(jnp.logical_not(can_recv(l, 7, d)))
        def _():
            YB[:, :, :, rows, :] = jnp.zeros((2, 12, 16, 4, 128), f32)

        @pl.when(jnp.logical_not(can_recv(q, 3, d)))
        def _():
            ZB[:, :, rows, :] = jnp.zeros((2, 12, 4, 128), f32)

        @pl.when(jnp.logical_not(can_recv(g, 15, d)))
        def _():
            for X in (FX, SX):
                X[pl.ds(0 if d else 16, 4)] = jnp.zeros((4, 16, 8, 128), f32)

    i8, c8 = iota((8, 256), 0), jnp.bitwise_and(iota((8, 256), 1), 127)
    SEL[...] = onehot(c8 == jnp.where(i8 < 4, i8, 120 + i8))

    for x in range(12):
        load(x).wait()

    pl.semaphore_wait(barrier, 31 + jnp.where(far, 1, 0))

    def send_edges(j, c):
        for p in (5 - j, 6 + j):
            for d in range(2):
                pl.when(can_send(l, 7, d))(lambda: ycopy(0, d, p).start())
        return c

    def send_planes(i, c):
        pl.when(can_send(g, 15, 1))(lambda: xcopy(0, 1, 3 - i).start())
        pl.when(can_send(g, 15, 0))(lambda: xcopy(0, 0, i).start())
        return c

    lax.fori_loop(0, 2, send_edges, 0)
    lax.fori_loop(0, 4, send_planes, 0)
    lax.fori_loop(2, 6, send_edges, 0)

    def first_z(x, c):
        ZS[0, x] = dot(SEL[...], both(FX[4 + x].reshape(128, 128)), NT)
        return c

    lax.fori_loop(0, 12, first_z, 0)
    for d in range(2):
        pl.when(can_send(q, 3, d))(lambda: z0copy(d).start())

    row, col = iota((128, 256), 0), iota((128, 256), 1)
    v, y = row >> 3, jnp.bitwise_and(row, 7)
    own = col < 128
    cc = jnp.bitwise_and(col, 127)
    w, s8 = cc >> 3, jnp.bitwise_and(cc, 7)
    y2 = jnp.where(own, s8, jnp.where(s8 < 4, 8 + s8, s8 - 8))
    rows_v = onehot(iota((128, 16), 0) >> 3 == iota((128, 16), 1))
    cols_w = onehot(jnp.bitwise_and(iota((16, 256), 1), 127) >> 3 == iota((16, 256), 0))

    def spread(value):
        total = jnp.zeros((128, 256), f32)
        for part in split(value):
            total = total + dot(dot(rows_v, part).astype(bf16), cols_w)
        return total

    lane = iota((16, 16), 1) == iota((16, 16), 0)

    def speed_rows(d):
        total = jnp.zeros((128, 256), f32)
        for part in split(jnp.where(lane, speeds_ref[d : d + 1, :], 0.0)):
            total = total + dot(rows_v, dot(part, jnp.ones((16, 256), bf16)).astype(bf16))
        return -TIME_STEP * total

    SXR[...] = speed_rows(0)[:, :128]
    SZR[...] = speed_rows(2)[:, :128]
    A = jnp.where(y == y2, TIME_STEP * spread(kin_ref[...]), 0.0)
    A = A + jnp.where(v == w, speed_rows(1) * stencil(y2 - y), 0.0)
    A2[...] = jnp.concatenate(split(A), axis=0)
    D = both(stencil(iota((128, 128), 0) - iota((128, 128), 1)))
    D2[...] = jnp.concatenate([D, D], axis=0)
    i8, z8 = iota((8, 128), 0), iota((8, 128), 1)
    E = both(stencil(jnp.where(i8 < 4, 128 + i8, i8 - 8) - z8))
    E2[...] = jnp.concatenate([E, E], axis=0)
    ZP[...] = jnp.zeros((128, 128), f32)
    ZP[:, 0:54] = zf_ref[...]
    Z2[...] = both(jnp.concatenate([ZP[...], pltpu.roll(ZP[...], 64, 1)], axis=0))

    XR[...] = jnp.zeros((16, 128), f32)
    for x in range(12):
        XR[x : x + 1, 0:96] = xf_ref[pl.ds(rank_ref[x], 1), :]
    YT[...] = jnp.zeros((8, 128), f32)
    YT[:, 0:64] = yf_ref[...]
    XG[g] = XR[...]
    YG[l] = YT[...]

    def xrow(peer, slot):
        return remote(XR, XG.at[slot], xrs.at[peer], xrr.at[slot], (peer, l, q))

    def yrow(peer, slot):
        return remote(YT, YG.at[slot], yrs.at[peer], yrr.at[slot], (g, peer, q))

    def over(n, me, act):
        def body(i, c):
            act(lax.rem(me + i, n))
            return c
        lax.fori_loop(1, n, body, 0)

    over(16, g, lambda peer: xrow(peer, g).start())
    over(8, l, lambda peer: yrow(peer, l).start())

    def change(X, s, p):
        center = X[4 + p].reshape(128, 128)
        F = jnp.concatenate([both(center), both(YB[s, p].reshape(128, 128))], axis=0)
        t = dot(A2[...], F)
        zt = dot(F[:128], D2[...])
        zt = zt + dot(jnp.concatenate(split(ZB[s, p]), axis=0), E2[...], TN)
        xt = jnp.zeros((16, 8, 128), f32)
        for i, c in enumerate(COEFFS):
            xt = xt + c * (X[5 + i + p] - X[3 - i + p])
        return center, quadrants(t) + SZR[...] * halves(zt) + SXR[...] * xt.reshape(128, 128)

    def wait_halo(j, s):
        for p in (5 - j, 6 + j):
            for d in range(2):
                pl.when(can_recv(l, 7, d))(lambda: ycopy(s, d, p).wait_recv())
                if s:
                    pl.when(can_recv(q, 3, d))(lambda: zcopy(d, p).wait_recv())
        for d in range(2):
            i = 5 - j if d else j - 2
            pl.when(jnp.logical_and(j >= 2, can_recv(g, 15, d)))(
                lambda: xcopy(s, d, i).wait_recv())

    for d in range(2):
        pl.when(can_recv(q, 3, d))(lambda: z0copy(d).wait_recv())

    def first(j, c):
        wait_halo(j, 0)
        for p in (5 - j, 6 + j):
            center, add = change(FX, 0, p)
            section = center + add
            SX[4 + p] = section.reshape(16, 8, 128)
            for d in range(2):
                pl.when(can_send(l, 7, d))(lambda: ycopy(1, d, p).start())
            ZS[1, p] = dot(SEL[...], both(section), NT)
            for d in range(2):
                pl.when(can_send(q, 3, d))(lambda: zcopy(d, p).start())
        for d in range(2):
            i = j - 2 if d else 5 - j
            pl.when(jnp.logical_and(j >= 2, can_send(g, 15, d)))(
                lambda: xcopy(1, d, i).start())
        return c

    lax.fori_loop(0, 6, first, 0)

    over(16, g, lambda peer: xrow(peer, peer).wait_recv())
    over(8, l, lambda peer: yrow(peer, peer).wait_recv())
    shape = (4, 12, 8, 256)
    src = 4 * iota(shape, 0) + (iota(shape, 2) >> 1)
    pick = onehot((16 * src + iota(shape, 1) == iota(shape, 3)).reshape(384, 256))
    shape = (6, 4, 8, 128)
    rank = 24 * iota(shape, 1) + 6 * (iota(shape, 2) >> 1) + iota(shape, 0)
    ranks = onehot((rank == iota(shape, 3)).reshape(192, 128))
    same = jnp.bitwise_and(iota((192, 384), 0) ^ iota((192, 384), 1), 1) == 0
    for n, part in enumerate(split(XG[...].reshape(256, 128))):
        rows = dot(ranks, dot(pick, part).astype(bf16), NT)
        X2[192 * n : 192 * n + 192, :] = jnp.where(same, rows, 0.0).astype(bf16)
    Y = YG[...].reshape(64, 128)
    Y = Y + pltpu.roll(Y, 64, 1)
    col = iota((64, 256), 1)
    pick = onehot(8 * jnp.bitwise_and(col >> 4, 7) + jnp.bitwise_and(col, 7) == iota((64, 256), 0))
    same = iota((128, 256), 0) >> 6 == jnp.bitwise_and(iota((128, 256), 1) >> 3, 1)
    for n, part in enumerate(split(Y)):
        W2[128 * n : 128 * n + 128, :] = jnp.where(same, dot(part, pick, TN), 0.0).astype(bf16)

    def put(p):
        return pltpu.make_async_copy(FN.at[p], next_ref.at[:, p], out_sem.at[p])

    def second(j, c):
        wait_halo(j, 1)
        for p in (5 - j, 6 + j):
            center, add = change(SX, 1, p)
            new = 0.5 * (FX[4 + p].reshape(128, 128) + center + add)
            FN[p] = new.reshape(16, 8, 128)
            put(p).start()
            new = new.reshape(8, 2, 8, 128)
            pair = jnp.concatenate([new[:, 0].reshape(64, 128), new[:, 1].reshape(64, 128)], axis=1)
            z = quadrants(dot(jnp.concatenate(split(pair), axis=0), Z2[...]))
            z = z.reshape(2, 2, 2, 8, 128)
            for n in range(2):
                PB[n, p] = z[:, n].reshape(4, 8, 128)
            bcopy(p).start()
        return c

    lax.fori_loop(0, 6, second, 0)

    def add_partner(x, c):
        bcopy(x).wait_recv()
        QB[x] = PB[k, x] + BR[x]
        return c

    lax.fori_loop(0, 12, add_partner, 0)

    def place(d):
        return d // 4, pl.ds(2 * lax.rem(d, 4), 2)

    def ccopy(peer, slot):
        t, rows = place(peer)
        t2, rows2 = place(slot)
        return remote(QB.at[:, t, rows], CT.at[t2, :, rows2], csend.at[peer], crecv.at[slot],
                      (peer, l, q))

    def ecopy(peer, slot):
        t, rows = place(peer)
        t2, rows2 = place(slot)
        return remote(RB.at[:, t, rows], EU.at[t2, :, rows2], esend.at[peer], erecv.at[slot],
                      (peer, l, q))

    t, rows = place(g)
    over(16, g, lambda peer: ccopy(peer, g).start())
    mine = pltpu.make_async_copy(QB.at[:, t, rows], CT.at[t, :, rows], own_sem.at[0])
    mine.start()
    mine.wait()
    over(16, g, lambda peer: ccopy(peer, peer).wait_recv())
    R = quadrants(dot(X2[...], both(CT[...].reshape(384, 128))))
    RB[...] = R.reshape(6, 4, 8, 128)
    over(16, g, lambda peer: ecopy(peer, g).start())
    mine = pltpu.make_async_copy(RB.at[:, t, rows], EU.at[t, :, rows], own_sem.at[1])
    mine.start()
    mine.wait()
    over(16, g, lambda peer: ecopy(peer, peer).wait_recv())

    units = [(u, a, b) for u in range(2) for a in range(3) for b in range(2)]

    def fcopy(unit):
        u, a, b = unit
        return remote(EU.at[2 * b + u, pl.ds(2 * a, 2)], FU.at[ring], fsend.at[8 * b + 3 * u + a],
                      frecv.at[ring], (g, 1 + 3 * u + a, 2 * b + k))

    def fcome(r):
        return remote(EU.at[0, pl.ds(0, 2)], FU.at[r], fsend.at[0], frecv.at[r], ring_device(r))

    def to_self(unit):
        u, a, b = unit
        return jnp.logical_and(l == 1 + 3 * u + a, h == b)

    for unit in units:
        pl.when(jnp.logical_not(to_self(unit)))(lambda: fcopy(unit).start())

        @pl.when(to_self(unit))
        def _():
            u, a, b = unit
            FU[ring] = EU[2 * b + u, pl.ds(2 * a, 2)]

    def gcopy(there, slot):
        return remote(SB.at[:, there], GB.at[slot], gsend.at[there], grecv.at[slot], (g, there, q))

    works = jnp.logical_and(l >= 1, l <= 6)

    @pl.when(works)
    def _():
        over(16, ring, lambda r: fcome(r).wait_recv())
        S = quadrants(dot(W2[...], both(FU[...].reshape(256, 128))))
        SB[...] = S.reshape(2, 8, 8, 128)
        over(8, l, lambda there: gcopy(there, l - 1).start())
        GB[l - 1] = SB[:, l]

    for e in range(6):
        pl.when(l != e + 1)(lambda: gcopy(l, e).wait_recv())
    for u in range(2):
        for a in range(6):
            tile = GB[3 * u + a // 2, a % 2]
            core_ref[2 * u, a] = tile[:, 0:54]
            core_ref[2 * u + 1, a] = pltpu.roll(tile, 64, 1)[:, 0:54]

    def done(p, c):
        for s in range(2):
            for d in range(2):
                pl.when(can_send(l, 7, d))(lambda: ycopy(s, d, p).wait_send())
        for d in range(2):
            pl.when(can_send(q, 3, d))(lambda: zcopy(d, p).wait_send())
        bcopy(p).wait_send()
        put(p).wait()
        return c

    lax.fori_loop(0, 12, done, 0)
    for d in range(2):
        pl.when(can_send(q, 3, d))(lambda: z0copy(d).wait_send())
        for s in range(2):
            for i in range(4):
                pl.when(can_send(g, 15, d))(lambda: xcopy(s, d, i).wait_send())

    def done_peer(peer):
        xrow(peer, g).wait_send()
        ccopy(peer, g).wait_send()
        ecopy(peer, g).wait_send()

    over(16, g, done_peer)
    over(8, l, lambda peer: yrow(peer, l).wait_send())
    for unit in units:
        pl.when(jnp.logical_not(to_self(unit)))(lambda: fcopy(unit).wait_send())

    @pl.when(works)
    def _():
        over(8, l, lambda there: gcopy(there, l - 1).wait_send())


def local(fields, speeds, kinetics, block_rank, x_factor, y_factor, z_factor):
    vmem, dma = pltpu.VMEM, pltpu.SemaphoreType.DMA
    in_vmem = pl.BlockSpec(memory_space=pltpu.VMEM)
    anywhere = pl.BlockSpec(memory_space=pl.ANY)
    return pl.pallas_call(
        kernel,
        out_shape=(
            jax.ShapeDtypeStruct(fields.shape, f32),
            jax.ShapeDtypeStruct((4, 6, 8, 54), f32),
        ),
        in_specs=[anywhere, in_vmem, in_vmem, pl.BlockSpec(memory_space=pltpu.SMEM)] + [in_vmem] * 3,
        out_specs=(anywhere, in_vmem),
        scratch_shapes=[
            vmem((20, 16, 8, 128), f32),
            vmem((20, 16, 8, 128), f32),
            vmem((2, 12, 16, 8, 128), f32),
            vmem((2, 12, 8, 128), f32),
            vmem((2, 12, 8, 128), f32),
            vmem((12, 16, 8, 128), f32),
            vmem((2, 12, 4, 8, 128), f32),
            vmem((12, 4, 8, 128), f32),
            vmem((12, 4, 8, 128), f32),
            vmem((4, 12, 8, 128), f32),
            vmem((6, 4, 8, 128), f32),
            vmem((4, 6, 8, 128), f32),
            vmem((16, 2, 8, 128), f32),
            vmem((2, 8, 8, 128), f32),
            vmem((6, 2, 8, 128), f32),
            vmem((16, 128), f32),
            vmem((16, 16, 128), f32),
            vmem((8, 128), f32),
            vmem((8, 8, 128), f32),
            vmem((128, 128), f32),
            vmem((256, 256), bf16),
            vmem((256, 256), bf16),
            vmem((16, 256), bf16),
            vmem((8, 256), bf16),
            vmem((256, 256), bf16),
            vmem((384, 384), bf16),
            vmem((256, 256), bf16),
            vmem((128, 128), f32),
            vmem((128, 128), f32),
            dma((12,)), dma((12,)), dma((2,)),
            dma((2, 2, 12)), dma((2, 2, 12)),
            dma((2, 12)), dma((2, 12)), dma((2,)), dma((2,)),
            dma((2, 2, 4)), dma((2, 2, 4)),
            dma((12,)), dma((12,)),
            dma((16,)), dma((16,)), dma((16,)), dma((16,)), dma((16,)), dma((16,)),
            dma((8,)), dma((8,)),
            dma((16,)), dma((16,)), dma((8,)), dma((8,)),
        ],
        compiler_params=pltpu.CompilerParams(
            collective_id=0, has_side_effects=True, vmem_limit_bytes=32 * 1024 * 1024),
    )(fields, speeds, kinetics, block_rank, x_factor, y_factor, z_factor)


def solution(mesh):
    placed = (P(None, "gx", "gy", "gz"), P(), P(), P("gx"), P(), P("gy", None), P("gz", None))
    return jax.shard_map(
        local,
        mesh=mesh,
        in_specs=placed,
        out_specs=(P(None, "gx", "gy", "gz"), P("gz", "gx", "gy", None)),
        check_vma=False,
    )
```

time: 214 us -> 80.6 us (0.38)
  Pallas kernels: 0 us -> 75.2 us
  starting transfers between devices: 64.4 us -> 0 us
  waiting for transfers between devices: 46.2 us -> 0 us
  blocking collectives: 43 us -> 0 us
  local copies, waits for them, and re-layouts: 33 us -> 4.43 us
  other arithmetic: 14.6 us -> 0 us
  matrix products: 9.96 us -> 0 us
    pallas_call x0 -> x1, Pallas kernels: none -> 75.2 us  [local(): pl.pallas_call(kernel, out_shape=(jax.ShapeDtypeStruct(fields.shape, f32)...]
    ppermute x12 -> x0, starting transfers between devices: 50.5 us -> none  [the longest x6 34.9 us: with_halo(): lax.ppermute(last, axis, up)]
    all_to_all x2 -> x0, blocking collectives: 43 us -> none  [sent_and_summed(): lax.all_to_all(pieces, axis, split_axis=0, concat_axis=0, tiled=True)]
    ppermute x12 -> x0, waiting for transfers between devices: 24 us -> none  [the longest x6 23.9 us: with_halo(): lax.ppermute(initial, axis, [(b, a) for a, b in up])]
    all_to_all x1 -> x0, waiting for transfers between devices: 22.2 us -> none  [sent_and_summed(): lax.all_to_all(pieces, axis, split_axis=0, concat_axis=0, tiled=True)]
    all_to_all x1 -> x0, starting transfers between devices: 13.9 us -> none  [sent_and_summed(): lax.all_to_all(pieces, axis, split_axis=0, concat_axis=0, tiled=True)]
    unnamed x31 -> x15, local copies, waits for them, and re-layouts: 16.7 us -> 4.43 us
    dot_general x6 -> x0, matrix products: 9.96 us -> none  [the longest x2 6.12 us: tendency(): jnp.einsum('vw,wxyz->vxyz', kinetics, center, precision=lax.Precision.HIG...]
  transfers between devices with their start and end apart: 13 -> 0, of which waited for: 3 -> 0; matrix products, arithmetic and copies ran while one was open for 9% -> 0% of each run, Pallas kernels for 0% -> 0%
where the time goes in v1:
time: 80.6 us; the launch traced here: 80.3 us
  Pallas kernels  75.2 us (93%)
  local copies, waits for them, and re-layouts  4.43 us (5%)
    pallas_call x1, Pallas kernels, local(): pl.pallas_call(kernel, out_shape=(jax.ShapeDtypeStruct(fields.shape, f32)...  75.2 us
    unnamed x15, local copies, waits for them, and re-layouts  4.43 us

profile of v1, /device:TPU:6, one launch (start us, length us, event | category | flops | bytes accessed | tf_op | source)
XLA Modules:
  0.0 80.3 jit_solution(15153414183719716831)
XLA Ops:
  0.6 0.0 copy-start.3
  0.6 0.0 copy-start.5
  0.7 0.0 copy-start.2
  0.7 0.0 copy-start.4
  0.7 0.9 %copy.9.zf_ref = f32[128,54]{1,0:T(8,128)S(1)} copy(f32[128,54]{0,1:T(8,128)} %param.13) | data formatting | bytes 55296 | tf_op args[6]
  1.5 0.0 copy-done.3
  1.5 0.0 copy-done.5
  1.6 0.0 copy-done.2
  1.6 0.0 copy-done.4
  1.6 0.0 copy-start
  1.6 1.1 %copy-done = f32[16,12,8,128]{3,2,1,0:T(8,128)S(1)} copy-done((f32[16,12,8,128]{3,2,1,0:T(8,128)S(1)}, f32[16,12,8,128]{3,2,1,0:T(8,128)}, u32[]{:S(2)}) %copy-start) | copy-done | bytes 786456
  2.7 0.0 copy-start.1
  2.7 0.9 %copy-done.1 = f32[192,96]{1,0:T(8,128)S(1)} copy-done((f32[192,96]{1,0:T(8,128)S(1)}, f32[192,96]{1,0:T(8,128)}, u32[]{:S(2)}) %copy-start.1) | copy-done | bytes 73752
  3.6 75.2 %shard_map.86 = (f32[16,12,8,128]{3,2,1,0:T(8,128)S(1)}, f32[4,6,8,54]{3,2,1,0:T(8,128)S(1)}) custom-call(f32[16,12,8,128]{3,2,1,0:T(8,128)S(1)} %copy-done, f32[3,16]{1,0:T(4,128)S(1)} %copy-done.4, f32[16,16]{1,0:T(8,128)S(1)} %copy-done.2, s32[12]{0:T(128)S(1)} %copy-done.5, f32[192,96]{1,0:T(8,128)S(1)} %copy-done.1, f32[8,64]{1,0:T(8,128)S(1)} %copy-done.3, ...), custom_call_target="tpu_custom_call" | custom-call | tf_op jit(solution)/shard_map/pallas_call | solution.py:441
  78.8 0.9 %copy.12 = f32[16,12,8,128]{3,2,1,0:T(8,128)} copy(f32[16,12,8,128]{3,2,1,0:T(8,128)S(1)} %get-tuple-element.4) | data formatting | bytes 1572864
  79.7 0.6 copy.13
Async XLA Ops:
  0.6 0.9 %copy-start.3 = (f32[8,64]{1,0:T(8,128)S(1)}, f32[8,64]{1,0:T(8,128)}, u32[]{:S(2)}) copy-start(f32[8,64]{1,0:T(8,128)} %yf_ref.1) | copy-start | bytes 6148
  0.6 0.9 %copy-start.5 = (s32[12]{0:T(128)S(1)}, s32[12]{0:T(128)}, u32[]{:S(2)}) copy-start(s32[12]{0:T(128)} %rank_ref.1) | copy-start | bytes 148
  0.7 0.9 %copy-start.2 = (f32[16,16]{1,0:T(8,128)S(1)}, f32[16,16]{1,0:T(8,128)}, u32[]{:S(2)}) copy-start(f32[16,16]{1,0:T(8,128)} %kin_ref.1) | copy-start | bytes 3076
  0.7 0.9 %copy-start.4 = (f32[3,16]{1,0:T(4,128)S(1)}, f32[3,16]{1,0:T(4,128)}, u32[]{:S(2)}) copy-start(f32[3,16]{1,0:T(4,128)} %speeds_ref.1) | copy-start | bytes 580
  1.6 1.1 %copy-start = (f32[16,12,8,128]{3,2,1,0:T(8,128)S(1)}, f32[16,12,8,128]{3,2,1,0:T(8,128)}, u32[]{:S(2)}) copy-start(f32[16,12,8,128]{3,2,1,0:T(8,128)} %f_ref.1) | copy-start | bytes 2359300
  2.7 0.9 %copy-start.1 = (f32[192,96]{1,0:T(8,128)S(1)}, f32[192,96]{1,0:T(8,128)}, u32[]{:S(2)}) copy-start(f32[192,96]{1,0:T(8,128)} %xf_ref.1) | copy-start | bytes 221188

commit v2 on v1

--- a/solution.py
+++ b/solution.py
@@ -54,13 +54,13 @@
 
 
 def kernel(
-    f_ref, speeds_ref, kin_ref, rank_ref, xf_ref, yf_ref, zf_ref,
+    f_hbm, speeds_hbm, kin_hbm, rank_hbm, xf_hbm, yf_hbm, zf_hbm,
     next_ref, core_ref,
-    FX, SX, YB, ZS, ZB, FN, PB, BR, QB, CT, RB, EU, FU, SB, GB, XR, XG, YT, YG, ZP,
+    FX, SX, YB, ZS, ZB, FN, PB, BR, QB, CT, RB, EU, FU, SB, GB, XR, XG, YT, YG, ZT, XF, YF, KIN, SPD, RANK,
     A2, D2, E2, SEL, Z2, X2, W2, SXR, SZR,
-    load_sem, out_sem, own_sem, ysend, yrecv, zsend, zrecv, z0send, z0recv, xsend, xrecv,
+    load_sem, small_sem, out_sem, own_sem, ysend, yrecv, zsend, zrecv, z0send, z0recv, xsend, xrecv,
     bsend, brecv, csend, crecv, esend, erecv, fsend, frecv, gsend, grecv,
-    xrs, xrr, yrs, yrr,
+    xrs, xrr, yrs, yrr, gx_round, z_round,
 ):
     g, l, q = lax.axis_index("gx"), lax.axis_index("gy"), lax.axis_index("gz")
     h, k = q // 2, lax.rem(q, 2)
@@ -76,7 +76,7 @@
             device_id=device, device_id_type=MESH)
 
     def load(x):
-        return pltpu.make_async_copy(f_ref.at[:, x], FX.at[4 + x], load_sem.at[x])
+        return pltpu.make_async_copy(f_hbm.at[:, x], FX.at[4 + x], load_sem.at[x])
 
     def ycopy(s, d, p):
         X = (FX, SX)[s]
@@ -109,27 +109,47 @@
     def can_recv(index, last, d):
         return index > 0 if d else index < last
 
-    for x in range(12):
-        load(x).start()
-
     barrier = pltpu.get_barrier_semaphore()
 
     def greet(device):
         pl.semaphore_signal(barrier, inc=1, device_id=device, device_id_type=MESH)
 
+    def gx_device(i):
+        return (lax.rem(g + i, 16), l, q)
+
     far = jnp.logical_or(q == 1, q == 2)
-
-    def greet_others(i, c):
-        greet((lax.rem(g + i, 16), l, q))
+    for i in (1, 15):
+        greet(gx_device(i))
         greet(ring_device(lax.rem(ring + i, 16)))
-        return c
-
     greet((g, l, partner))
-    lax.fori_loop(1, 16, greet_others, 0)
 
     @pl.when(far)
     def _():
         greet((g, l, 3 - q))
+
+    for x in range(12):
+        load(x).start()
+    small = [
+        pltpu.make_async_copy(src, dst, small_sem.at[i])
+        for i, (src, dst) in enumerate((
+            (speeds_hbm, SPD), (kin_hbm, KIN), (rank_hbm, RANK), (xf_hbm, XF),
+            (yf_hbm, YF), (zf_hbm, ZT.at[pl.ds(0, 54)]),
+        ))
+    ]
+    YT[...] = jnp.zeros((8, 128), f32)
+    ZT[...] = jnp.zeros((64, 128), f32)
+    for copy in small:
+        copy.start()
+
+    def tell(n):
+        for i in (1 << n, 16 - (1 << n)):
+            pl.semaphore_signal(gx_round.at[n], inc=1, device_id=gx_device(i), device_id_type=MESH)
+            pl.semaphore_signal(z_round.at[n], inc=1, device_id=ring_device(lax.rem(ring + i, 16)),
+                                device_id_type=MESH)
+
+    def hear(n):
+        pl.semaphore_wait(gx_round.at[n], 2)
+        pl.semaphore_wait(z_round.at[n], 2)
 
     for d in range(2):
         rows = pl.ds(4 * d, 4)
@@ -149,11 +169,17 @@
 
     i8, c8 = iota((8, 256), 0), jnp.bitwise_and(iota((8, 256), 1), 127)
     SEL[...] = onehot(c8 == jnp.where(i8 < 4, i8, 120 + i8))
-
     for x in range(12):
         load(x).wait()
 
-    pl.semaphore_wait(barrier, 31 + jnp.where(far, 1, 0))
+    def first_z(x, c):
+        ZS[0, x] = dot(SEL[...], both(FX[4 + x].reshape(128, 128)), NT)
+        return c
+
+    lax.fori_loop(0, 12, first_z, 0)
+    pl.semaphore_wait(barrier, 5 + jnp.where(far, 1, 0))
+    for d in range(2):
+        pl.when(can_send(q, 3, d))(lambda: z0copy(d).start())
 
     def send_edges(j, c):
         for p in (5 - j, 6 + j):
@@ -169,14 +195,9 @@
     lax.fori_loop(0, 2, send_edges, 0)
     lax.fori_loop(0, 4, send_planes, 0)
     lax.fori_loop(2, 6, send_edges, 0)
-
-    def first_z(x, c):
-        ZS[0, x] = dot(SEL[...], both(FX[4 + x].reshape(128, 128)), NT)
-        return c
-
-    lax.fori_loop(0, 12, first_z, 0)
-    for d in range(2):
-        pl.when(can_send(q, 3, d))(lambda: z0copy(d).start())
+    tell(0)
+    for copy in small:
+        copy.wait()
 
     row, col = iota((128, 256), 0), iota((128, 256), 1)
     v, y = row >> 3, jnp.bitwise_and(row, 7)
@@ -197,13 +218,13 @@
 
     def speed_rows(d):
         total = jnp.zeros((128, 256), f32)
-        for part in split(jnp.where(lane, speeds_ref[d : d + 1, :], 0.0)):
+        for part in split(jnp.where(lane, SPD[d : d + 1, :], 0.0)):
             total = total + dot(rows_v, dot(part, jnp.ones((16, 256), bf16)).astype(bf16))
         return -TIME_STEP * total
 
     SXR[...] = speed_rows(0)[:, :128]
     SZR[...] = speed_rows(2)[:, :128]
-    A = jnp.where(y == y2, TIME_STEP * spread(kin_ref[...]), 0.0)
+    A = jnp.where(y == y2, TIME_STEP * spread(KIN[...]), 0.0)
     A = A + jnp.where(v == w, speed_rows(1) * stencil(y2 - y), 0.0)
     A2[...] = jnp.concatenate(split(A), axis=0)
     D = both(stencil(iota((128, 128), 0) - iota((128, 128), 1)))
@@ -211,15 +232,15 @@
     i8, z8 = iota((8, 128), 0), iota((8, 128), 1)
     E = both(stencil(jnp.where(i8 < 4, 128 + i8, i8 - 8) - z8))
     E2[...] = jnp.concatenate([E, E], axis=0)
-    ZP[...] = jnp.zeros((128, 128), f32)
-    ZP[:, 0:54] = zf_ref[...]
-    Z2[...] = both(jnp.concatenate([ZP[...], pltpu.roll(ZP[...], 64, 1)], axis=0))
+    Z = ZT[...]
+    none = jnp.zeros((64, 128), f32)
+    Z = jnp.concatenate([jnp.concatenate([Z, none], axis=1), jnp.concatenate([none, Z], axis=1)], axis=0)
+    Z2[...] = jnp.concatenate(split(Z), axis=0)
 
     XR[...] = jnp.zeros((16, 128), f32)
-    for x in range(12):
-        XR[x : x + 1, 0:96] = xf_ref[pl.ds(rank_ref[x], 1), :]
-    YT[...] = jnp.zeros((8, 128), f32)
-    YT[:, 0:64] = yf_ref[...]
+    for i in range(12):
+        XR[i : i + 1, 0:96] = XF[pl.ds(RANK[6 + i // 2 if i % 2 else 5 - i // 2], 1), :]
+    YT[:, 0:64] = YF[...]
     XG[g] = XR[...]
     YG[l] = YT[...]
 
@@ -235,8 +256,8 @@
             return c
         lax.fori_loop(1, n, body, 0)
 
-    over(16, g, lambda peer: xrow(peer, g).start())
-    over(8, l, lambda peer: yrow(peer, l).start())
+    hear(0)
+    tell(1)
 
     def change(X, s, p):
         center = X[4 + p].reshape(128, 128)
@@ -264,16 +285,20 @@
         pl.when(can_recv(q, 3, d))(lambda: z0copy(d).wait_recv())
 
     def first(j, c):
+        @pl.when(j == 2)
+        def _():
+            hear(1)
+            tell(2)
+
         wait_halo(j, 0)
         for p in (5 - j, 6 + j):
             center, add = change(FX, 0, p)
             section = center + add
             SX[4 + p] = section.reshape(16, 8, 128)
-            for d in range(2):
-                pl.when(can_send(l, 7, d))(lambda: ycopy(1, d, p).start())
             ZS[1, p] = dot(SEL[...], both(section), NT)
             for d in range(2):
                 pl.when(can_send(q, 3, d))(lambda: zcopy(d, p).start())
+                pl.when(can_send(l, 7, d))(lambda: ycopy(1, d, p).start())
         for d in range(2):
             i = j - 2 if d else 5 - j
             pl.when(jnp.logical_and(j >= 2, can_send(g, 15, d)))(
@@ -282,62 +307,76 @@
 
     lax.fori_loop(0, 6, first, 0)
 
-    over(16, g, lambda peer: xrow(peer, peer).wait_recv())
-    over(8, l, lambda peer: yrow(peer, peer).wait_recv())
-    shape = (4, 12, 8, 256)
-    src = 4 * iota(shape, 0) + (iota(shape, 2) >> 1)
-    pick = onehot((16 * src + iota(shape, 1) == iota(shape, 3)).reshape(384, 256))
-    shape = (6, 4, 8, 128)
-    rank = 24 * iota(shape, 1) + 6 * (iota(shape, 2) >> 1) + iota(shape, 0)
-    ranks = onehot((rank == iota(shape, 3)).reshape(192, 128))
-    same = jnp.bitwise_and(iota((192, 384), 0) ^ iota((192, 384), 1), 1) == 0
-    for n, part in enumerate(split(XG[...].reshape(256, 128))):
-        rows = dot(ranks, dot(pick, part).astype(bf16), NT)
-        X2[192 * n : 192 * n + 192, :] = jnp.where(same, rows, 0.0).astype(bf16)
-    Y = YG[...].reshape(64, 128)
-    Y = Y + pltpu.roll(Y, 64, 1)
-    col = iota((64, 256), 1)
-    pick = onehot(8 * jnp.bitwise_and(col >> 4, 7) + jnp.bitwise_and(col, 7) == iota((64, 256), 0))
-    same = iota((128, 256), 0) >> 6 == jnp.bitwise_and(iota((128, 256), 1) >> 3, 1)
-    for n, part in enumerate(split(Y)):
-        W2[128 * n : 128 * n + 128, :] = jnp.where(same, dot(part, pick, TN), 0.0).astype(bf16)
+    hear(2)
+    over(16, g, lambda peer: xrow(peer, g).start())
+    over(8, l, lambda peer: yrow(peer, l).start())
+
+    def projections():
+        over(16, g, lambda peer: xrow(peer, peer).wait_recv())
+        over(8, l, lambda peer: yrow(peer, peer).wait_recv())
+        shape = (4, 12, 8, 256)
+        src = 4 * iota(shape, 0) + (iota(shape, 2) >> 1)
+        pick = onehot((16 * src + iota(shape, 1) == iota(shape, 3)).reshape(384, 256))
+        shape = (6, 4, 8, 128)
+        rank = 24 * iota(shape, 1) + 6 * (iota(shape, 2) >> 1) + iota(shape, 0)
+        ranks = onehot((rank == iota(shape, 3)).reshape(192, 128))
+        same = jnp.bitwise_and(iota((192, 384), 0) ^ iota((192, 384), 1), 1) == 0
+        for n, part in enumerate(split(XG[...].reshape(256, 128))):
+            rows = dot(ranks, dot(pick, part).astype(bf16), NT)
+            X2[192 * n : 192 * n + 192, :] = jnp.where(same, rows, 0.0).astype(bf16)
+        Y = YG[...].reshape(64, 128)
+        Y = Y + pltpu.roll(Y, 64, 1)
+        col = iota((64, 256), 1)
+        pick = onehot(8 * jnp.bitwise_and(col >> 4, 7) + jnp.bitwise_and(col, 7) == iota((64, 256), 0))
+        same = iota((128, 256), 0) >> 6 == jnp.bitwise_and(iota((128, 256), 1) >> 3, 1)
+        for n, part in enumerate(split(Y)):
+            W2[128 * n : 128 * n + 128, :] = jnp.where(same, dot(part, pick, TN), 0.0).astype(bf16)
 
     def put(p):
         return pltpu.make_async_copy(FN.at[p], next_ref.at[:, p], out_sem.at[p])
 
+    def place(d):
+        return d // 4, pl.ds(2 * lax.rem(d, 4), 2)
+
+    def ccopy(n, peer, slot):
+        t, rows = place(peer)
+        t2, rows2 = place(slot)
+        part = pl.ds(8 * n, 8 - 4 * n)
+        return remote(QB.at[part, t, rows], CT.at[t2, part, rows2], csend.at[n, peer],
+                      crecv.at[n, slot], (peer, l, q))
+
+    def send_part(n):
+        def add_partner(x, c):
+            bcopy(x).wait_recv()
+            QB[x] = PB[k, x] + BR[x]
+            return c
+
+        lax.fori_loop(8 * n, 8 + 4 * n, add_partner, 0)
+        over(16, g, lambda peer: ccopy(n, peer, g).start())
+
     def second(j, c):
         wait_halo(j, 1)
-        for p in (5 - j, 6 + j):
+        for i, p in enumerate((5 - j, 6 + j)):
             center, add = change(SX, 1, p)
             new = 0.5 * (FX[4 + p].reshape(128, 128) + center + add)
             FN[p] = new.reshape(16, 8, 128)
             put(p).start()
             new = new.reshape(8, 2, 8, 128)
             pair = jnp.concatenate([new[:, 0].reshape(64, 128), new[:, 1].reshape(64, 128)], axis=1)
-            z = quadrants(dot(jnp.concatenate(split(pair), axis=0), Z2[...]))
+            z = quadrants(dot(jnp.concatenate(split(pair), axis=0), Z2[...], NT))
             z = z.reshape(2, 2, 2, 8, 128)
             for n in range(2):
-                PB[n, p] = z[:, n].reshape(4, 8, 128)
-            bcopy(p).start()
+                PB[n, 2 * j + i] = z[:, n].reshape(4, 8, 128)
+            bcopy(2 * j + i).start()
         return c
 
-    lax.fori_loop(0, 6, second, 0)
-
-    def add_partner(x, c):
-        bcopy(x).wait_recv()
-        QB[x] = PB[k, x] + BR[x]
-        return c
-
-    lax.fori_loop(0, 12, add_partner, 0)
-
-    def place(d):
-        return d // 4, pl.ds(2 * lax.rem(d, 4), 2)
-
-    def ccopy(peer, slot):
-        t, rows = place(peer)
-        t2, rows2 = place(slot)
-        return remote(QB.at[:, t, rows], CT.at[t2, :, rows2], csend.at[peer], crecv.at[slot],
-                      (peer, l, q))
+    lax.fori_loop(0, 4, second, 0)
+    projections()
+    second(4, 0)
+    send_part(0)
+    second(5, 0)
+
+    send_part(1)
 
     def ecopy(peer, slot):
         t, rows = place(peer)
@@ -346,11 +385,11 @@
                       (peer, l, q))
 
     t, rows = place(g)
-    over(16, g, lambda peer: ccopy(peer, g).start())
     mine = pltpu.make_async_copy(QB.at[:, t, rows], CT.at[t, :, rows], own_sem.at[0])
     mine.start()
     mine.wait()
-    over(16, g, lambda peer: ccopy(peer, peer).wait_recv())
+    for n in range(2):
+        over(16, g, lambda peer: ccopy(n, peer, peer).wait_recv())
     R = quadrants(dot(X2[...], both(CT[...].reshape(384, 128))))
     RB[...] = R.reshape(6, 4, 8, 128)
     over(16, g, lambda peer: ecopy(peer, g).start())
@@ -421,7 +460,8 @@
 
     def done_peer(peer):
         xrow(peer, g).wait_send()
-        ccopy(peer, g).wait_send()
+        for n in range(2):
+            ccopy(n, peer, g).wait_send()
         ecopy(peer, g).wait_send()
 
     over(16, g, done_peer)
@@ -437,15 +477,15 @@
 def local(fields, speeds, kinetics, block_rank, x_factor, y_factor, z_factor):
     vmem, dma = pltpu.VMEM, pltpu.SemaphoreType.DMA
     in_vmem = pl.BlockSpec(memory_space=pltpu.VMEM)
-    anywhere = pl.BlockSpec(memory_space=pl.ANY)
+    in_hbm = pl.BlockSpec(memory_space=pltpu.HBM)
     return pl.pallas_call(
         kernel,
         out_shape=(
             jax.ShapeDtypeStruct(fields.shape, f32),
             jax.ShapeDtypeStruct((4, 6, 8, 54), f32),
         ),
-        in_specs=[anywhere, in_vmem, in_vmem, pl.BlockSpec(memory_space=pltpu.SMEM)] + [in_vmem] * 3,
-        out_specs=(anywhere, in_vmem),
+        in_specs=[in_hbm] * 7,
+        out_specs=(in_hbm, in_vmem),
         scratch_shapes=[
             vmem((20, 16, 8, 128), f32),
             vmem((20, 16, 8, 128), f32),
@@ -466,7 +506,12 @@
             vmem((16, 16, 128), f32),
             vmem((8, 128), f32),
             vmem((8, 8, 128), f32),
-            vmem((128, 128), f32),
+            vmem((64, 128), f32),
+            vmem((192, 96), f32),
+            vmem((8, 64), f32),
+            vmem((16, 16), f32),
+            vmem((3, 16), f32),
+            pltpu.SMEM((12,), jnp.int32),
             vmem((256, 256), bf16),
             vmem((256, 256), bf16),
             vmem((16, 256), bf16),
@@ -476,18 +521,19 @@
             vmem((256, 256), bf16),
             vmem((128, 128), f32),
             vmem((128, 128), f32),
-            dma((12,)), dma((12,)), dma((2,)),
+            dma((12,)), dma((6,)), dma((12,)), dma((2,)),
             dma((2, 2, 12)), dma((2, 2, 12)),
             dma((2, 12)), dma((2, 12)), dma((2,)), dma((2,)),
             dma((2, 2, 4)), dma((2, 2, 4)),
             dma((12,)), dma((12,)),
-            dma((16,)), dma((16,)), dma((16,)), dma((16,)), dma((16,)), dma((16,)),
+            dma((2, 16)), dma((2, 16)), dma((16,)), dma((16,)), dma((16,)), dma((16,)),
             dma((8,)), dma((8,)),
             dma((16,)), dma((16,)), dma((8,)), dma((8,)),
+            pltpu.SemaphoreType.REGULAR((3,)), pltpu.SemaphoreType.REGULAR((3,)),
         ],
         compiler_params=pltpu.CompilerParams(
-            collective_id=0, has_side_effects=True, vmem_limit_bytes=32 * 1024 * 1024),
-    )(fields, speeds, kinetics, block_rank, x_factor, y_factor, z_factor)
+            collective_id=0, has_side_effects=True, vmem_limit_bytes=60 * 1024 * 1024),
+    )(fields, speeds, kinetics, block_rank, x_factor, y_factor, z_factor.T)
 
 
 def solution(mesh):

time: 80.6 us -> 75.3 us (0.934)
  Pallas kernels: 75.2 us -> 71.1 us
  local copies, waits for them, and re-layouts: 4.43 us -> 2.75 us
    pallas_call x1, Pallas kernels: 75.2 us -> 71.1 us  [local(): pl.pallas_call(kernel, out_shape=(jax.ShapeDtypeStruct(fields.shape, f32)...]
    unnamed x15 -> x4, local copies, waits for them, and re-layouts: 4.43 us -> 2.75 us
where the time goes in v2:
time: 75.3 us; the launch traced here: 74.5 us
  Pallas kernels  71.1 us (94%)
  local copies, waits for them, and re-layouts  2.75 us (4%)
    pallas_call x1, Pallas kernels, local(): pl.pallas_call(kernel, out_shape=(jax.ShapeDtypeStruct(fields.shape, f32)...  71.1 us
    unnamed x4, local copies, waits for them, and re-layouts  2.75 us

profile of v2, /device:TPU:6, one launch (start us, length us, event | category | flops | bytes accessed | tf_op | source)
XLA Modules:
  0.0 74.5 jit_solution(6813129951798145324)
XLA Ops:
  0.6 71.1 %shard_map.86 = (f32[16,12,8,128]{3,2,1,0:T(8,128)}, f32[4,6,8,54]{3,2,1,0:T(8,128)}) custom-call(f32[16,12,8,128]{3,2,1,0:T(8,128)} %f_hbm.1, f32[3,16]{1,0:T(4,128)} %speeds_hbm.1, f32[16,16]{1,0:T(8,128)} %kin_hbm.1, s32[12]{0:T(128)} %rank_hbm.1, f32[192,96]{1,0:T(8,128)} %xf_hbm.1, f32[8,64]{1,0:T(8,128)} %yf_hbm.1, f32[54,128]{1,0:T(8,128)} %bitcast.1), custom_call_target="tpu_custom_call" | custom-call | tf_op jit(solution)/shard_map/pallas_call | solution.py:481
  71.7 0.0 copy-start
  71.7 2.1 %copy.11 = f32[16,12,8,128]{3,2,1,0:T(8,128)} copy(f32[16,12,8,128]{3,2,1,0:T(8,128)} %get-tuple-element.4) | data formatting | bytes 1572864
  73.8 0.0 copy-done
  73.8 0.6 copy.12
Async XLA Ops:
  71.7 2.1 %copy-start = (f32[4,6,8,54]{3,2,1,0:T(8,128)S(1)}, f32[4,6,8,54]{3,2,1,0:T(8,128)}, u32[]{:S(2)}) copy-start(f32[4,6,8,54]{3,2,1,0:T(8,128)} %get-tuple-element.5) | copy-start | bytes 124420

commit v3 on v2

--- a/solution.py
+++ b/solution.py
@@ -53,12 +53,25 @@
     return jnp.concatenate(split(a), axis=1)
 
 
+def stacked(a):
+    return jnp.concatenate(split(a), axis=0)
+
+
+def product(a, b):
+    return quadrants(dot(stacked(a), both(b)))
+
+
+def paired(a):
+    a = a.reshape(8, 2, 8, 128)
+    return jnp.concatenate([a[:, 0].reshape(64, 128), a[:, 1].reshape(64, 128)], axis=1)
+
+
 def kernel(
     f_hbm, speeds_hbm, kin_hbm, rank_hbm, xf_hbm, yf_hbm, zf_hbm,
     next_ref, core_ref,
-    FX, SX, YB, ZS, ZB, FN, PB, BR, QB, CT, RB, EU, FU, SB, GB, XR, XG, YT, YG, ZT, XF, YF, KIN, SPD, RANK,
-    A2, D2, E2, SEL, Z2, X2, W2, SXR, SZR,
-    load_sem, small_sem, out_sem, own_sem, ysend, yrecv, zsend, zrecv, z0send, z0recv, xsend, xrecv,
+    FX, SX, YB, ZS, ZB, FN, PB, BR, QB, CT, RB, EU, FU, SB, GB, XR, XG, YT, YG, ZT, ZE, ZX, XF, YF, KIN, SPD, RANK,
+    A2, K2, D2, E2, SEL, Z2, X2, W2, SXR, SZR,
+    load_sem, small_sem, out_sem, own_sem, ysend, yrecv, zsend, zrecv, z0send, z0recv, zfsend, zfrecv, xsend, xrecv,
     bsend, brecv, csend, crecv, esend, erecv, fsend, frecv, gsend, grecv,
     xrs, xrr, yrs, yrr, gx_round, z_round,
 ):
@@ -87,6 +100,10 @@
     def z0copy(d):
         rows = pl.ds(4 * d, 4)
         return remote(ZS.at[0, :, rows], ZB.at[0, :, rows], z0send.at[d], z0recv.at[d],
+                      (g, l, q + 2 * d - 1))
+
+    def zfcopy(d):
+        return remote(ZE.at[pl.ds(4 * d, 4)], ZX.at[pl.ds(128 + 4 * d, 4)], zfsend.at[d], zfrecv.at[d],
                       (g, l, q + 2 * d - 1))
 
     def zcopy(d, p):
@@ -137,7 +154,8 @@
         ))
     ]
     YT[...] = jnp.zeros((8, 128), f32)
-    ZT[...] = jnp.zeros((64, 128), f32)
+    ZT[...] = jnp.zeros((128, 128), f32)
+    ZX[pl.ds(136, 120)] = jnp.zeros((120, 128), f32)
     for copy in small:
         copy.start()
 
@@ -161,6 +179,7 @@
         @pl.when(jnp.logical_not(can_recv(q, 3, d)))
         def _():
             ZB[:, :, rows, :] = jnp.zeros((2, 12, 4, 128), f32)
+            ZX[pl.ds(128 + 4 * d, 4)] = jnp.zeros((4, 128), f32)
 
         @pl.when(jnp.logical_not(can_recv(g, 15, d)))
         def _():
@@ -177,9 +196,15 @@
         return c
 
     lax.fori_loop(0, 12, first_z, 0)
+    for copy in small:
+        copy.wait()
+    ZX[pl.ds(0, 128)] = ZT[...].T
+    ZE[pl.ds(0, 4)] = ZX[pl.ds(0, 4)]
+    ZE[pl.ds(4, 4)] = ZX[pl.ds(124, 4)]
     pl.semaphore_wait(barrier, 5 + jnp.where(far, 1, 0))
     for d in range(2):
         pl.when(can_send(q, 3, d))(lambda: z0copy(d).start())
+        pl.when(can_send(q, 3, d))(lambda: zfcopy(d).start())
 
     def send_edges(j, c):
         for p in (5 - j, 6 + j):
@@ -196,8 +221,6 @@
     lax.fori_loop(0, 4, send_planes, 0)
     lax.fori_loop(2, 6, send_edges, 0)
     tell(0)
-    for copy in small:
-        copy.wait()
 
     row, col = iota((128, 256), 0), iota((128, 256), 1)
     v, y = row >> 3, jnp.bitwise_and(row, 7)
@@ -225,6 +248,7 @@
     SXR[...] = speed_rows(0)[:, :128]
     SZR[...] = speed_rows(2)[:, :128]
     A = jnp.where(y == y2, TIME_STEP * spread(KIN[...]), 0.0)
+    K2[...] = stacked(A[:, :128])
     A = A + jnp.where(v == w, speed_rows(1) * stencil(y2 - y), 0.0)
     A2[...] = jnp.concatenate(split(A), axis=0)
     D = both(stencil(iota((128, 128), 0) - iota((128, 128), 1)))
@@ -232,11 +256,6 @@
     i8, z8 = iota((8, 128), 0), iota((8, 128), 1)
     E = both(stencil(jnp.where(i8 < 4, 128 + i8, i8 - 8) - z8))
     E2[...] = jnp.concatenate([E, E], axis=0)
-    Z = ZT[...]
-    none = jnp.zeros((64, 128), f32)
-    Z = jnp.concatenate([jnp.concatenate([Z, none], axis=1), jnp.concatenate([none, Z], axis=1)], axis=0)
-    Z2[...] = jnp.concatenate(split(Z), axis=0)
-
     XR[...] = jnp.zeros((16, 128), f32)
     for i in range(12):
         XR[i : i + 1, 0:96] = XF[pl.ds(RANK[6 + i // 2 if i % 2 else 5 - i // 2], 1), :]
@@ -258,6 +277,8 @@
 
     hear(0)
     tell(1)
+    hear(1)
+    tell(2)
 
     def change(X, s, p):
         center = X[4 + p].reshape(128, 128)
@@ -283,33 +304,40 @@
 
     for d in range(2):
         pl.when(can_recv(q, 3, d))(lambda: z0copy(d).wait_recv())
+        pl.when(can_recv(q, 3, d))(lambda: zfcopy(d).wait_recv())
+
+    row, col = iota((128, 256), 0), iota((128, 256), 1)
+    Z = ZX[pl.ds(0, 128)]
+    DZ = product(stencil(row - jnp.where(col < 132, col, col - 136)), ZX[...])
+    for n, a in enumerate((Z, DZ)):
+        Z2[256 * n : 256 * n + 256, :] = both(jnp.concatenate([a, pltpu.roll(a, 64, 1)], axis=0))
 
     def first(j, c):
-        @pl.when(j == 2)
+        @pl.when(j == 4)
         def _():
-            hear(1)
-            tell(2)
+            hear(2)
+            over(16, g, lambda peer: xrow(peer, g).start())
+            over(8, l, lambda peer: yrow(peer, l).start())
 
         wait_halo(j, 0)
-        for p in (5 - j, 6 + j):
+        for i, p in enumerate((5 - j, 6 + j)):
             center, add = change(FX, 0, p)
             section = center + add
             SX[4 + p] = section.reshape(16, 8, 128)
-            ZS[1, p] = dot(SEL[...], both(section), NT)
+            parts = both(section)
+            ZS[1, p] = dot(SEL[...], parts, NT)
+            mixed = 0.5 * (FX[4 + p].reshape(128, 128) + section + quadrants(dot(K2[...], parts)))
+            both_z = jnp.concatenate([paired(mixed), paired(0.5 * SZR[...] * section)], axis=1)
+            z0 = quadrants(dot(stacked(both_z), Z2[...])).reshape(2, 2, 2, 8, 128)
+            z1 = quadrants(dot(stacked(paired(section)), Z2[0:256, :])).reshape(2, 2, 2, 8, 128)
+            for n in range(2):
+                PB[n, 2 * j + i, 0] = z0[:, n].reshape(4, 8, 128)
+                PB[n, 2 * j + i, 1] = z1[:, n].reshape(4, 8, 128)
+            bcopy(2 * j + i).start()
             for d in range(2):
                 pl.when(can_send(q, 3, d))(lambda: zcopy(d, p).start())
                 pl.when(can_send(l, 7, d))(lambda: ycopy(1, d, p).start())
-        for d in range(2):
-            i = j - 2 if d else 5 - j
-            pl.when(jnp.logical_and(j >= 2, can_send(g, 15, d)))(
-                lambda: xcopy(1, d, i).start())
-        return c
-
-    lax.fori_loop(0, 6, first, 0)
-
-    hear(2)
-    over(16, g, lambda peer: xrow(peer, g).start())
-    over(8, l, lambda peer: yrow(peer, l).start())
+        return c
 
     def projections():
         over(16, g, lambda peer: xrow(peer, peer).wait_recv())
@@ -321,16 +349,26 @@
         rank = 24 * iota(shape, 1) + 6 * (iota(shape, 2) >> 1) + iota(shape, 0)
         ranks = onehot((rank == iota(shape, 3)).reshape(192, 128))
         same = jnp.bitwise_and(iota((192, 384), 0) ^ iota((192, 384), 1), 1) == 0
-        for n, part in enumerate(split(XG[...].reshape(256, 128))):
-            rows = dot(ranks, dot(pick, part).astype(bf16), NT)
-            X2[192 * n : 192 * n + 192, :] = jnp.where(same, rows, 0.0).astype(bf16)
+        def plane(index):
+            step, n = jnp.bitwise_and(index, 15) >> 1, jnp.bitwise_and(index, 1)
+            return 12 * (index >> 4) + jnp.where(n == 1, 6 + step, 5 - step)
+
+        X = XG[...].reshape(256, 128)
+        DX = product(stencil(plane(iota((256, 256), 0)) - plane(iota((256, 256), 1))), X)
+        for m, a in enumerate((X, DX)):
+            for n, part in enumerate(split(a)):
+                rows = dot(ranks, dot(pick, part).astype(bf16), NT)
+                X2[192 * n : 192 * n + 192, 384 * m : 384 * m + 384] = jnp.where(same, rows, 0.0).astype(bf16)
         Y = YG[...].reshape(64, 128)
         Y = Y + pltpu.roll(Y, 64, 1)
+        DY = product(stencil(iota((64, 64), 0) - iota((64, 64), 1)), Y)
         col = iota((64, 256), 1)
         pick = onehot(8 * jnp.bitwise_and(col >> 4, 7) + jnp.bitwise_and(col, 7) == iota((64, 256), 0))
         same = iota((128, 256), 0) >> 6 == jnp.bitwise_and(iota((128, 256), 1) >> 3, 1)
-        for n, part in enumerate(split(Y)):
-            W2[128 * n : 128 * n + 128, :] = jnp.where(same, dot(part, pick, TN), 0.0).astype(bf16)
+        for m, a in enumerate((Y, DY)):
+            for n, part in enumerate(split(a)):
+                W2[128 * n : 128 * n + 128, 256 * m : 256 * m + 256] = (
+                    jnp.where(same, dot(part, pick, TN), 0.0).astype(bf16))
 
     def put(p):
         return pltpu.make_async_copy(FN.at[p], next_ref.at[:, p], out_sem.at[p])
@@ -342,7 +380,7 @@
         t, rows = place(peer)
         t2, rows2 = place(slot)
         part = pl.ds(8 * n, 8 - 4 * n)
-        return remote(QB.at[part, t, rows], CT.at[t2, part, rows2], csend.at[n, peer],
+        return remote(QB.at[part, :, t, rows], CT.at[t2, part, :, rows2], csend.at[n, peer],
                       crecv.at[n, slot], (peer, l, q))
 
     def send_part(n):
@@ -356,90 +394,101 @@
 
     def second(j, c):
         wait_halo(j, 1)
-        for i, p in enumerate((5 - j, 6 + j)):
+        for p in (5 - j, 6 + j):
             center, add = change(SX, 1, p)
             new = 0.5 * (FX[4 + p].reshape(128, 128) + center + add)
             FN[p] = new.reshape(16, 8, 128)
             put(p).start()
-            new = new.reshape(8, 2, 8, 128)
-            pair = jnp.concatenate([new[:, 0].reshape(64, 128), new[:, 1].reshape(64, 128)], axis=1)
-            z = quadrants(dot(jnp.concatenate(split(pair), axis=0), Z2[...], NT))
-            z = z.reshape(2, 2, 2, 8, 128)
-            for n in range(2):
-                PB[n, 2 * j + i] = z[:, n].reshape(4, 8, 128)
-            bcopy(2 * j + i).start()
-        return c
-
-    lax.fori_loop(0, 4, second, 0)
+        return c
+
+    lax.fori_loop(0, 5, first, 0)
+    send_part(0)
+    first(5, 0)
+
+    send_part(1)
     projections()
-    second(4, 0)
-    send_part(0)
-    second(5, 0)
-
-    send_part(1)
 
     def ecopy(peer, slot):
         t, rows = place(peer)
         t2, rows2 = place(slot)
-        return remote(RB.at[:, t, rows], EU.at[t2, :, rows2], esend.at[peer], erecv.at[slot],
+        return remote(RB.at[:, :, t, rows], EU.at[:, t2, :, rows2], esend.at[peer], erecv.at[slot],
                       (peer, l, q))
 
     t, rows = place(g)
-    mine = pltpu.make_async_copy(QB.at[:, t, rows], CT.at[t, :, rows], own_sem.at[0])
+    mine = pltpu.make_async_copy(QB.at[:, :, t, rows], CT.at[t, :, :, rows], own_sem.at[0])
     mine.start()
     mine.wait()
     for n in range(2):
         over(16, g, lambda peer: ccopy(n, peer, peer).wait_recv())
-    R = quadrants(dot(X2[...], both(CT[...].reshape(384, 128))))
-    RB[...] = R.reshape(6, 4, 8, 128)
+    v0 = 8 * (t // 2) + 4 * k + 2 * lax.rem(t, 2)
+
+    def lane_speeds(d):
+        which = iota((1, 16), 1)
+        pair = [jnp.sum(jnp.where(which == v0 + n, SPD[d : d + 1, :], 0.0), axis=1, keepdims=True)
+                for n in range(2)]
+        return -0.5 * TIME_STEP * jnp.where(iota((1, 128), 1) < 64, pair[0], pair[1])
+
+    T0, T1 = CT[:, :, 0].reshape(384, 128), CT[:, :, 1].reshape(384, 128)
+    R0 = quadrants(dot(X2[...], both(jnp.concatenate([T0, lane_speeds(0) * T1], axis=0))))
+    R1 = quadrants(dot(X2[:, 0:384], both(lane_speeds(1) * T1)))
+    RB[0] = R0.reshape(6, 4, 8, 128)
+    RB[1] = R1.reshape(6, 4, 8, 128)
     over(16, g, lambda peer: ecopy(peer, g).start())
-    mine = pltpu.make_async_copy(RB.at[:, t, rows], EU.at[t, :, rows], own_sem.at[1])
+
+    def send_sections(i, c):
+        pl.when(can_send(g, 15, 1))(lambda: xcopy(1, 1, 3 - i).start())
+        pl.when(can_send(g, 15, 0))(lambda: xcopy(1, 0, i).start())
+        return c
+
+    lax.fori_loop(0, 4, send_sections, 0)
+    mine = pltpu.make_async_copy(RB.at[:, :, t, rows], EU.at[:, t, :, rows], own_sem.at[1])
     mine.start()
     mine.wait()
+    lax.fori_loop(0, 2, second, 0)
     over(16, g, lambda peer: ecopy(peer, peer).wait_recv())
 
-    units = [(u, a, b) for u in range(2) for a in range(3) for b in range(2)]
-
-    def fcopy(unit):
-        u, a, b = unit
-        return remote(EU.at[2 * b + u, pl.ds(2 * a, 2)], FU.at[ring], fsend.at[8 * b + 3 * u + a],
-                      frecv.at[ring], (g, 1 + 3 * u + a, 2 * b + k))
+    def unit(r):
+        n = lax.rem(r, 8) - 1
+        return 2 * (r // 8) + n // 3, pl.ds(2 * lax.rem(n, 3), 2)
+
+    def working(r):
+        return jnp.logical_and(lax.rem(r, 8) >= 1, lax.rem(r, 8) <= 6)
+
+    def fcopy(r):
+        t, ranks = unit(r)
+        return remote(EU.at[:, t, ranks], FU.at[ring], fsend.at[r], frecv.at[ring], ring_device(r))
 
     def fcome(r):
-        return remote(EU.at[0, pl.ds(0, 2)], FU.at[r], fsend.at[0], frecv.at[r], ring_device(r))
-
-    def to_self(unit):
-        u, a, b = unit
-        return jnp.logical_and(l == 1 + 3 * u + a, h == b)
-
-    for unit in units:
-        pl.when(jnp.logical_not(to_self(unit)))(lambda: fcopy(unit).start())
-
-        @pl.when(to_self(unit))
-        def _():
-            u, a, b = unit
-            FU[ring] = EU[2 * b + u, pl.ds(2 * a, 2)]
+        return remote(EU.at[:, 0, pl.ds(0, 2)], FU.at[r], fsend.at[r], frecv.at[r], ring_device(r))
+
+    def send_unit(i, c):
+        r = lax.rem(ring + jnp.where(lax.rem(i, 2) == 0, 8 + i // 2, 7 - i // 2), 16)
+        pl.when(working(r))(lambda: fcopy(r).start())
+        return c
+
+    lax.fori_loop(0, 15, send_unit, 0)
+    works = working(ring)
+
+    @pl.when(works)
+    def _():
+        t, ranks = unit(ring)
+        mine = pltpu.make_async_copy(EU.at[:, t, ranks], FU.at[ring], own_sem.at[0])
+        mine.start()
+        mine.wait()
 
     def gcopy(there, slot):
         return remote(SB.at[:, there], GB.at[slot], gsend.at[there], grecv.at[slot], (g, there, q))
 
-    works = jnp.logical_and(l >= 1, l <= 6)
+    lax.fori_loop(2, 6, second, 0)
 
     @pl.when(works)
     def _():
         over(16, ring, lambda r: fcome(r).wait_recv())
-        S = quadrants(dot(W2[...], both(FU[...].reshape(256, 128))))
+        U = [FU[:, n].reshape(256, 128) for n in range(2)]
+        S = quadrants(dot(W2[...], both(jnp.concatenate(U, axis=0))))
         SB[...] = S.reshape(2, 8, 8, 128)
         over(8, l, lambda there: gcopy(there, l - 1).start())
         GB[l - 1] = SB[:, l]
-
-    for e in range(6):
-        pl.when(l != e + 1)(lambda: gcopy(l, e).wait_recv())
-    for u in range(2):
-        for a in range(6):
-            tile = GB[3 * u + a // 2, a % 2]
-            core_ref[2 * u, a] = tile[:, 0:54]
-            core_ref[2 * u + 1, a] = pltpu.roll(tile, 64, 1)[:, 0:54]
 
     def done(p, c):
         for s in range(2):
@@ -454,6 +503,7 @@
     lax.fori_loop(0, 12, done, 0)
     for d in range(2):
         pl.when(can_send(q, 3, d))(lambda: z0copy(d).wait_send())
+        pl.when(can_send(q, 3, d))(lambda: zfcopy(d).wait_send())
         for s in range(2):
             for i in range(4):
                 pl.when(can_send(g, 15, d))(lambda: xcopy(s, d, i).wait_send())
@@ -466,8 +516,15 @@
 
     over(16, g, done_peer)
     over(8, l, lambda peer: yrow(peer, l).wait_send())
-    for unit in units:
-        pl.when(jnp.logical_not(to_self(unit)))(lambda: fcopy(unit).wait_send())
+    over(16, ring, lambda r: pl.when(working(r))(lambda: fcopy(r).wait_send()))
+
+    for e in range(6):
+        pl.when(l != e + 1)(lambda: gcopy(l, e).wait_recv())
+    for u in range(2):
+        for a in range(6):
+            tile = GB[3 * u + a // 2, a % 2]
+            core_ref[2 * u, a] = tile[:, 0:54]
+            core_ref[2 * u + 1, a] = pltpu.roll(tile, 64, 1)[:, 0:54]
 
     @pl.when(works)
     def _():
@@ -493,37 +550,40 @@
             vmem((2, 12, 8, 128), f32),
             vmem((2, 12, 8, 128), f32),
             vmem((12, 16, 8, 128), f32),
-            vmem((2, 12, 4, 8, 128), f32),
-            vmem((12, 4, 8, 128), f32),
-            vmem((12, 4, 8, 128), f32),
-            vmem((4, 12, 8, 128), f32),
-            vmem((6, 4, 8, 128), f32),
-            vmem((4, 6, 8, 128), f32),
-            vmem((16, 2, 8, 128), f32),
+            vmem((2, 12, 2, 4, 8, 128), f32),
+            vmem((12, 2, 4, 8, 128), f32),
+            vmem((12, 2, 4, 8, 128), f32),
+            vmem((4, 12, 2, 8, 128), f32),
+            vmem((2, 6, 4, 8, 128), f32),
+            vmem((2, 4, 6, 8, 128), f32),
+            vmem((16, 2, 2, 8, 128), f32),
             vmem((2, 8, 8, 128), f32),
             vmem((6, 2, 8, 128), f32),
             vmem((16, 128), f32),
             vmem((16, 16, 128), f32),
             vmem((8, 128), f32),
             vmem((8, 8, 128), f32),
-            vmem((64, 128), f32),
+            vmem((128, 128), f32),
+            vmem((8, 128), f32),
+            vmem((256, 128), f32),
             vmem((192, 96), f32),
             vmem((8, 64), f32),
             vmem((16, 16), f32),
             vmem((3, 16), f32),
             pltpu.SMEM((12,), jnp.int32),
             vmem((256, 256), bf16),
+            vmem((256, 128), bf16),
             vmem((256, 256), bf16),
             vmem((16, 256), bf16),
             vmem((8, 256), bf16),
-            vmem((256, 256), bf16),
-            vmem((384, 384), bf16),
-            vmem((256, 256), bf16),
+            vmem((512, 256), bf16),
+            vmem((384, 768), bf16),
+            vmem((256, 512), bf16),
             vmem((128, 128), f32),
             vmem((128, 128), f32),
             dma((12,)), dma((6,)), dma((12,)), dma((2,)),
             dma((2, 2, 12)), dma((2, 2, 12)),
-            dma((2, 12)), dma((2, 12)), dma((2,)), dma((2,)),
+            dma((2, 12)), dma((2, 12)), dma((2,)), dma((2,)), dma((2,)), dma((2,)),
             dma((2, 2, 4)), dma((2, 2, 4)),
             dma((12,)), dma((12,)),
             dma((2, 16)), dma((2, 16)), dma((16,)), dma((16,)), dma((16,)), dma((16,)),

time: 75.3 us -> 71.8 us (0.954)
  Pallas kernels: 71.1 us -> 68.2 us
    pallas_call x1, Pallas kernels: 71.1 us -> 68.2 us  [local(): pl.pallas_call(kernel, out_shape=(jax.ShapeDtypeStruct(fields.shape, f32)...]
where the time goes in v3:
time: 71.8 us; the launch traced here: 71.6 us
  Pallas kernels  68.2 us (95%)
  local copies, waits for them, and re-layouts  2.75 us (4%)
    pallas_call x1, Pallas kernels, local(): pl.pallas_call(kernel, out_shape=(jax.ShapeDtypeStruct(fields.shape, f32)...  68.2 us
    unnamed x4, local copies, waits for them, and re-layouts  2.75 us

profile of v3, /device:TPU:6, one launch (start us, length us, event | category | flops | bytes accessed | tf_op | source)
XLA Modules:
  0.0 71.6 jit_solution(15963331351998936522)
XLA Ops:
  0.6 68.2 %shard_map.86 = (f32[16,12,8,128]{3,2,1,0:T(8,128)}, f32[4,6,8,54]{3,2,1,0:T(8,128)}) custom-call(f32[16,12,8,128]{3,2,1,0:T(8,128)} %f_hbm.1, f32[3,16]{1,0:T(4,128)} %speeds_hbm.1, f32[16,16]{1,0:T(8,128)} %kin_hbm.1, s32[12]{0:T(128)} %rank_hbm.1, f32[192,96]{1,0:T(8,128)} %xf_hbm.1, f32[8,64]{1,0:T(8,128)} %yf_hbm.1, f32[54,128]{1,0:T(8,128)} %bitcast.1), custom_call_target="tpu_custom_call" | custom-call | tf_op jit(solution)/shard_map/pallas_call | solution.py:538
  68.9 0.0 copy-start
  68.9 2.1 %copy.11 = f32[16,12,8,128]{3,2,1,0:T(8,128)} copy(f32[16,12,8,128]{3,2,1,0:T(8,128)} %get-tuple-element.4) | data formatting | bytes 1572864
  71.0 0.0 copy-done
  71.0 0.6 copy.12
Async XLA Ops:
  68.9 2.1 %copy-start = (f32[4,6,8,54]{3,2,1,0:T(8,128)S(1)}, f32[4,6,8,54]{3,2,1,0:T(8,128)}, u32[]{:S(2)}) copy-start(f32[4,6,8,54]{3,2,1,0:T(8,128)} %get-tuple-element.5) | copy-start | bytes 124420

commit v4 on v3

--- a/solution.py
+++ b/solution.py
@@ -106,9 +106,9 @@
         return remote(ZE.at[pl.ds(4 * d, 4)], ZX.at[pl.ds(128 + 4 * d, 4)], zfsend.at[d], zfrecv.at[d],
                       (g, l, q + 2 * d - 1))
 
-    def zcopy(d, p):
-        rows = pl.ds(4 * d, 4)
-        return remote(ZS.at[1, p, rows], ZB.at[1, p, rows], zsend.at[d, p], zrecv.at[d, p],
+    def zcopy(d, j):
+        rows, pair = pl.ds(4 * d, 4), pl.ds(2 * j, 2)
+        return remote(ZS.at[1, pair, rows], ZB.at[1, pair, rows], zsend.at[d, j], zrecv.at[d, j],
                       (g, l, q + 2 * d - 1))
 
     def xcopy(s, d, i):
@@ -118,7 +118,8 @@
                       (g + 2 * d - 1, l, q))
 
     def bcopy(x):
-        return remote(PB.at[1 - k, x], BR.at[x], bsend.at[x], brecv.at[x], (g, l, partner))
+        pair = pl.ds(2 * x, 2)
+        return remote(PB.at[1 - k, pair], BR.at[pair], bsend.at[x], brecv.at[x], (g, l, partner))
 
     def can_send(index, last, d):
         return index < last if d else index > 0
@@ -192,7 +193,8 @@
         load(x).wait()
 
     def first_z(x, c):
-        ZS[0, x] = dot(SEL[...], both(FX[4 + x].reshape(128, 128)), NT)
+        p = jnp.where(lax.rem(x, 2) == 1, 6 + x // 2, 5 - x // 2)
+        ZS[0, x] = dot(SEL[...], both(FX[4 + p].reshape(128, 128)), NT)
         return c
 
     lax.fori_loop(0, 12, first_z, 0)
@@ -280,12 +282,12 @@
     hear(1)
     tell(2)
 
-    def change(X, s, p):
+    def change(X, s, p, place):
         center = X[4 + p].reshape(128, 128)
         F = jnp.concatenate([both(center), both(YB[s, p].reshape(128, 128))], axis=0)
         t = dot(A2[...], F)
         zt = dot(F[:128], D2[...])
-        zt = zt + dot(jnp.concatenate(split(ZB[s, p]), axis=0), E2[...], TN)
+        zt = zt + dot(jnp.concatenate(split(ZB[s, place]), axis=0), E2[...], TN)
         xt = jnp.zeros((16, 8, 128), f32)
         for i, c in enumerate(COEFFS):
             xt = xt + c * (X[5 + i + p] - X[3 - i + p])
@@ -295,9 +297,9 @@
         for p in (5 - j, 6 + j):
             for d in range(2):
                 pl.when(can_recv(l, 7, d))(lambda: ycopy(s, d, p).wait_recv())
-                if s:
-                    pl.when(can_recv(q, 3, d))(lambda: zcopy(d, p).wait_recv())
         for d in range(2):
+            if s:
+                pl.when(can_recv(q, 3, d))(lambda: zcopy(d, j).wait_recv())
             i = 5 - j if d else j - 2
             pl.when(jnp.logical_and(j >= 2, can_recv(g, 15, d)))(
                 lambda: xcopy(s, d, i).wait_recv())
@@ -321,11 +323,11 @@
 
         wait_halo(j, 0)
         for i, p in enumerate((5 - j, 6 + j)):
-            center, add = change(FX, 0, p)
+            center, add = change(FX, 0, p, 2 * j + i)
             section = center + add
             SX[4 + p] = section.reshape(16, 8, 128)
             parts = both(section)
-            ZS[1, p] = dot(SEL[...], parts, NT)
+            ZS[1, 2 * j + i] = dot(SEL[...], parts, NT)
             mixed = 0.5 * (FX[4 + p].reshape(128, 128) + section + quadrants(dot(K2[...], parts)))
             both_z = jnp.concatenate([paired(mixed), paired(0.5 * SZR[...] * section)], axis=1)
             z0 = quadrants(dot(stacked(both_z), Z2[...])).reshape(2, 2, 2, 8, 128)
@@ -333,9 +335,11 @@
             for n in range(2):
                 PB[n, 2 * j + i, 0] = z0[:, n].reshape(4, 8, 128)
                 PB[n, 2 * j + i, 1] = z1[:, n].reshape(4, 8, 128)
-            bcopy(2 * j + i).start()
+        bcopy(j).start()
+        for d in range(2):
+            pl.when(can_send(q, 3, d))(lambda: zcopy(d, j).start())
+        for p in (5 - j, 6 + j):
             for d in range(2):
-                pl.when(can_send(q, 3, d))(lambda: zcopy(d, p).start())
                 pl.when(can_send(l, 7, d))(lambda: ycopy(1, d, p).start())
         return c
 
@@ -386,16 +390,17 @@
     def send_part(n):
         def add_partner(x, c):
             bcopy(x).wait_recv()
-            QB[x] = PB[k, x] + BR[x]
+            pair = pl.ds(2 * x, 2)
+            QB[pair] = PB[k, pair] + BR[pair]
             return c
 
-        lax.fori_loop(8 * n, 8 + 4 * n, add_partner, 0)
+        lax.fori_loop(4 * n, 4 + 2 * n, add_partner, 0)
         over(16, g, lambda peer: ccopy(n, peer, g).start())
 
     def second(j, c):
         wait_halo(j, 1)
-        for p in (5 - j, 6 + j):
-            center, add = change(SX, 1, p)
+        for i, p in enumerate((5 - j, 6 + j)):
+            center, add = change(SX, 1, p, 2 * j + i)
             new = 0.5 * (FX[4 + p].reshape(128, 128) + center + add)
             FN[p] = new.reshape(16, 8, 128)
             put(p).start()
@@ -494,13 +499,14 @@
         for s in range(2):
             for d in range(2):
                 pl.when(can_send(l, 7, d))(lambda: ycopy(s, d, p).wait_send())
+        put(p).wait()
+        return c
+
+    lax.fori_loop(0, 12, done, 0)
+    for j in range(6):
+        bcopy(j).wait_send()
         for d in range(2):
-            pl.when(can_send(q, 3, d))(lambda: zcopy(d, p).wait_send())
-        bcopy(p).wait_send()
-        put(p).wait()
-        return c
-
-    lax.fori_loop(0, 12, done, 0)
+            pl.when(can_send(q, 3, d))(lambda: zcopy(d, j).wait_send())
     for d in range(2):
         pl.when(can_send(q, 3, d))(lambda: z0copy(d).wait_send())
         pl.when(can_send(q, 3, d))(lambda: zfcopy(d).wait_send())
@@ -583,9 +589,9 @@
             vmem((128, 128), f32),
             dma((12,)), dma((6,)), dma((12,)), dma((2,)),
             dma((2, 2, 12)), dma((2, 2, 12)),
-            dma((2, 12)), dma((2, 12)), dma((2,)), dma((2,)), dma((2,)), dma((2,)),
+            dma((2, 6)), dma((2, 6)), dma((2,)), dma((2,)), dma((2,)), dma((2,)),
             dma((2, 2, 4)), dma((2, 2, 4)),
-            dma((12,)), dma((12,)),
+            dma((6,)), dma((6,)),
             dma((2, 16)), dma((2, 16)), dma((16,)), dma((16,)), dma((16,)), dma((16,)),
             dma((8,)), dma((8,)),
             dma((16,)), dma((16,)), dma((8,)), dma((8,)),

time: 71.8 us -> 70.7 us (0.985)
  Pallas kernels: 68.2 us -> 66.5 us
    pallas_call x1, Pallas kernels: 68.2 us -> 66.5 us  [local(): pl.pallas_call(kernel, out_shape=(jax.ShapeDtypeStruct(fields.shape, f32)...]
where the time goes in v4:
time: 70.7 us; the launch traced here: 69.9 us
  Pallas kernels  66.5 us (94%)
  local copies, waits for them, and re-layouts  2.75 us (4%)
    pallas_call x1, Pallas kernels, local(): pl.pallas_call(kernel, out_shape=(jax.ShapeDtypeStruct(fields.shape, f32)...  66.5 us
    unnamed x4, local copies, waits for them, and re-layouts  2.75 us

profile of v4, /device:TPU:6, one launch (start us, length us, event | category | flops | bytes accessed | tf_op | source)
XLA Modules:
  0.0 69.9 jit_solution(793480477524191816)
XLA Ops:
  0.6 66.5 %shard_map.86 = (f32[16,12,8,128]{3,2,1,0:T(8,128)}, f32[4,6,8,54]{3,2,1,0:T(8,128)}) custom-call(f32[16,12,8,128]{3,2,1,0:T(8,128)} %f_hbm.1, f32[3,16]{1,0:T(4,128)} %speeds_hbm.1, f32[16,16]{1,0:T(8,128)} %kin_hbm.1, s32[12]{0:T(128)} %rank_hbm.1, f32[192,96]{1,0:T(8,128)} %xf_hbm.1, f32[8,64]{1,0:T(8,128)} %yf_hbm.1, f32[54,128]{1,0:T(8,128)} %bitcast.1), custom_call_target="tpu_custom_call" | custom-call | tf_op jit(solution)/shard_map/pallas_call | solution.py:544
  67.2 0.0 copy-start
  67.2 2.1 %copy.11 = f32[16,12,8,128]{3,2,1,0:T(8,128)} copy(f32[16,12,8,128]{3,2,1,0:T(8,128)} %get-tuple-element.4) | data formatting | bytes 1572864
  69.3 0.0 copy-done
  69.3 0.6 copy.12
Async XLA Ops:
  67.2 2.1 %copy-start = (f32[4,6,8,54]{3,2,1,0:T(8,128)S(1)}, f32[4,6,8,54]{3,2,1,0:T(8,128)}, u32[]{:S(2)}) copy-start(f32[4,6,8,54]{3,2,1,0:T(8,128)} %get-tuple-element.5) | copy-start | bytes 124420

commit v5 on v4

--- a/solution.py
+++ b/solution.py
@@ -273,9 +273,9 @@
 
     def over(n, me, act):
         def body(i, c):
-            act(lax.rem(me + i, n))
+            act(lax.rem(me + n // 2 + jnp.where(lax.rem(i, 2) == 0, i // 2, -((i + 1) // 2)), n))
             return c
-        lax.fori_loop(1, n, body, 0)
+        lax.fori_loop(0, n - 1, body, 0)
 
     hear(0)
     tell(1)

time: 70.7 us -> 70.1 us (level)
  no operation moved by 1% of the time
where the time goes in v5:
time: 70.1 us; the launch traced here: 70 us
  Pallas kernels  66.6 us (95%)
  local copies, waits for them, and re-layouts  2.75 us (4%)
    pallas_call x1, Pallas kernels, local(): pl.pallas_call(kernel, out_shape=(jax.ShapeDtypeStruct(fields.shape, f32)...  66.6 us
    unnamed x4, local copies, waits for them, and re-layouts  2.75 us

profile of v5, /device:TPU:6, one launch (start us, length us, event | category | flops | bytes accessed | tf_op | source)
XLA Modules:
  0.0 70.0 jit_solution(15164508182156817815)
XLA Ops:
  0.6 66.6 %shard_map.86 = (f32[16,12,8,128]{3,2,1,0:T(8,128)}, f32[4,6,8,54]{3,2,1,0:T(8,128)}) custom-call(f32[16,12,8,128]{3,2,1,0:T(8,128)} %f_hbm.1, f32[3,16]{1,0:T(4,128)} %speeds_hbm.1, f32[16,16]{1,0:T(8,128)} %kin_hbm.1, s32[12]{0:T(128)} %rank_hbm.1, f32[192,96]{1,0:T(8,128)} %xf_hbm.1, f32[8,64]{1,0:T(8,128)} %yf_hbm.1, f32[54,128]{1,0:T(8,128)} %bitcast.1), custom_call_target="tpu_custom_call" | custom-call | tf_op jit(solution)/shard_map/pallas_call | solution.py:544
  67.2 0.0 copy-start
  67.2 2.1 %copy.11 = f32[16,12,8,128]{3,2,1,0:T(8,128)} copy(f32[16,12,8,128]{3,2,1,0:T(8,128)} %get-tuple-element.4) | data formatting | bytes 1572864
  69.3 0.0 copy-done
  69.3 0.6 copy.12
Async XLA Ops:
  67.2 2.1 %copy-start = (f32[4,6,8,54]{3,2,1,0:T(8,128)S(1)}, f32[4,6,8,54]{3,2,1,0:T(8,128)}, u32[]{:S(2)}) copy-start(f32[4,6,8,54]{3,2,1,0:T(8,128)} %get-tuple-element.5) | copy-start | bytes 124420
